TPU v7x, 512 devices: a whole 4x8x8 slice. The times are simulated.
512 devices in a mesh: hst: 64 (over z, y_lo, core), dev: 8 (over y_hi, x).
Axes of the slice: x: 4, y: 8 (y_hi: 2, y_lo: 4; y = y_hi * 4 + y_lo), z: 8, core: 2. Of those that a mesh axis runs over, the one named last changes fastest.
Arguments:
- grad_out: bfloat16 [65536, 12288], P(('hst', 'dev')), may hold values from -24 to 24
- pre_act: bfloat16 [65536, 64], P(('hst', 'dev')), may hold values from -6 to 6
- down_rows: bfloat16 [12288, 64], P(('hst', 'dev')), may hold values from -0.0546875 to 0.0546875
- states: float32 [3, 163840, 128], P(None, ('hst', 'dev')), may hold values from -6 to 6
- partner_hosts: int32 [64, 2], replicated, may hold values from 0 to 63, as said below
- slice_start: int32 [64, 8], P('hst', 'dev'), may hold values from 0 to 64, as said below
Outputs:
- grad_bucket: float32 [12288, 64], P(('hst', 'dev'))
- grad_pre: bfloat16 [65536, 64], P(('hst', 'dev'))
- backup: float32 [3, 2, 131072, 128], P(None, None, ('hst', 'dev'))
Inputs may be any that keep to these rules, and one draw needn't show every extreme that they name: Each column is a permutation of the hosts; partner_hosts[h, 0], partner_hosts[h, 1] and h are three different hosts. `slice_start`: every entry is a multiple of 8.
All inputs are finite; a program needn't handle non-finite values.
Results may differ from a plain program's by a relative error of at most 0.0027.
Values may be sent and summed in bfloat16 or wider, within the bound.
No kernel may reach another device: no remote copies, remote signals or barrier semaphores. Data moves between devices by JAX's collectives and lax.ppermute only.
A program may use at most 64 MiB of HBM per device.

v0:
```python
import jax
import jax.numpy as jnp
from jax import lax
from jax.sharding import PartitionSpec as P

CKR = 256


def gelu_value(inputs):
    cubic = inputs * inputs * inputs
    tangent = jnp.tanh(0.7978845608 * (inputs + 0.044715 * cubic))
    return 0.5 * inputs * (1.0 + tangent)


def gelu_slope(inputs):
    squared = inputs * inputs
    tangent = jnp.tanh(0.7978845608 * (inputs + 0.044715 * squared * inputs))
    return 0.5 * (1.0 + tangent) + 0.5 * inputs * (1.0 - tangent * tangent) * 0.7978845608 * (
        1.0 + 3.0 * 0.044715 * squared
    )


def shards(grad_out, pre_act, down_rows, states, partner_hosts, slice_start):
    host_count = lax.axis_size("hst")
    local_count = lax.axis_size("dev")
    device_count = host_count * local_count
    lane_count = states.shape[2]
    pre_float = pre_act.astype(jnp.float32)
    activation = gelu_value(pre_float).astype(jnp.bfloat16)
    backward = jnp.dot(
        grad_out,
        lax.all_gather(down_rows, ("hst", "dev"), axis=0, tiled=True),
        preferred_element_type=jnp.float32,
    )
    grad_pre = (backward * gelu_slope(pre_float)).astype(jnp.bfloat16)
    term = jnp.einsum("td,tr->dr", grad_out, activation, preferred_element_type=jnp.float32)
    summed = lax.psum_scatter(term, ("hst", "dev"), scatter_dimension=0, tiled=True)
    grad_bucket = summed / device_count
    first_row = slice_start[0, 0]
    own_slice = lax.dynamic_slice_in_dim(states, first_row, CKR, 1)
    block_rows = CKR // host_count
    spread = lax.all_to_all(
        own_slice.reshape(3, host_count, block_rows, lane_count),
        "hst",
        split_axis=1,
        concat_axis=1,
        tiled=True,
    )
    sources = jnp.arange(host_count, dtype=jnp.int32)
    matches = partner_hosts[:, :, None] == sources[None, None, :]
    inverse = jnp.sum(jnp.where(matches, sources[:, None, None], 0), axis=0)
    outgoing = jnp.take(spread, inverse, axis=1)
    arrived = lax.all_to_all(outgoing, "hst", split_axis=2, concat_axis=2, tiled=True)
    backup = arrived.reshape(3, 2, CKR, lane_count)
    return (grad_bucket, grad_pre, backup)


def solution(mesh):
    return jax.shard_map(
        shards,
        mesh=mesh,
        in_specs=(
            P(("hst", "dev"), None),
            P(("hst", "dev"), None),
            P(("hst", "dev"), None),
            P(None, ("hst", "dev"), None),
            P(),
            P("hst", "dev"),
        ),
        out_specs=(
            P(("hst", "dev"), None),
            P(("hst", "dev"), None),
            P(None, None, ("hst", "dev"), None),
        ),
        check_vma=False,
    )
```

profile of v0, /device:TPU:1, one launch (start us, length us, event | category | flops | bytes accessed | tf_op | source)
XLA Modules:
  0.0 1697.9 jit_solution(597101506199957694)
XLA Ops:
  7.2 0.0 all-reduce.3.cloned.1.call-start
  7.2 1.8 copy-done
  9.1 3.0 convolution_bitcast_fusion
  12.1 0.0 all-reduce.3.cloned.1.call-update
  12.1 0.0 all-gather.2.cloned.1.call-start
  12.1 0.7 all-gather.2.cloned.1.call-update
  13.5 1.0 constant_dynamic-slice_fusion
  14.5 0.8 copy.27
  15.3 15.6 all-to-all-start
  30.9 0.1 select_reduce_fusion
  31.0 0.1 reshape.35
  31.1 0.7 copy.26
  31.8 0.6 pad_clamp_fusion
  32.4 15.2 all-to-all-done
  47.6 1.1 copy.28
  48.7 2.2 gather_fusion
  50.9 2.3 fusion.1
  53.2 5.2 all-to-all-start.1
  58.5 256.8 %all-reduce.3.cloned.1.call-done = f32[12288,64]{0,1:T(8,128)} async-done(((f32[12288,64]{0,1:T(8,128)}), f32[12288,64]{0,1:T(8,128)}) %all-reduce.3.cloned.1.call-update) | async-done | bytes 3145744
  315.3 0.9 dynamic-slice_multiply_fusion
  316.2 0.7 copy.31
  316.8 2.1 copy.30
  319.0 1368.1 %all-gather.2.cloned.1.call-done = bf16[12288,64]{1,0:T(8,128)(2,1)} async-done(((bf16[24,64]{1,0:T(8,128)(2,1)}), bf16[12288,64]{1,0:T(8,128)(2,1)}) %all-gather.2.cloned.1.call-update) | async-done | bytes 1572880 | tf_op jit(solution)/shard_map/all_gather | solution.py:32
  1687.1 3.9 fusion
  (8 shorter events, 0.0 us)
Async XLA Ops:
  7.2 1.9 copy-start
  7.2 308.1 %all-reduce.3.cloned.1.call-start = ((), (), s32[]{:S(2)}) async-start(), calls=%async_computation.3 | async-start | bytes 6291456
  12.0 18.9 %copy-start.2 = (s32[64,2]{0,1:T(2,128)S(1)}, s32[64,2]{0,1:T(2,128)}, u32[]{:S(2)}) copy-start(s32[64,2]{0,1:T(2,128)} %param.10) | copy-start | bytes 1540
  12.1 1675.0 %all-gather.2.cloned.1.call-start = ((), (), s32[]{:S(2)}) async-start(), calls=%async_computation.2 | async-start | bytes 3151872 | tf_op jit(solution)/shard_map/all_gather | solution.py:32
  15.3 32.3 %all-to-all-start = ((f32[3,64,4,128]{3,2,0,1:T(4,128)}), f32[3,64,4,128]{3,2,0,1:T(4,128)}, u32[]{:S(2)}, u32[]{:S(2)}) async-start(f32[3,64,4,128]{3,2,0,1:T(4,128)} %copy.27), calls=%async_computation | async-start | bytes 786432 | tf_op jit(solution)/shard_map/all_to_all | solution.py:42
  48.7 1638.4 %copy-start.1 = (bf16[128,64]{0,1:T(8,128)(2,1)S(1)}, bf16[128,64]{0,1:T(8,128)(2,1)}, u32[]{:S(2)}) copy-start(bf16[128,64]{0,1:T(8,128)(2,1)} %param.7) | copy-start | bytes 49156
  53.2 263.6 %all-to-all-start.1 = ((f32[3,2,64,4,128]{4,3,0,1,2:T(4,128)}), f32[3,2,64,4,128]{4,3,0,1,2:T(4,128)}, u32[]{:S(2)}, u32[]{:S(2)}) async-start(f32[3,2,64,4,128]{4,3,0,1,2:T(4,128)} %fusion.1), calls=%async_computation.1 | async-start | bytes 1572864 | tf_op jit(solution)/shard_map/all_to_all | solution.py:53
Sparse Core Ops, SparseCore 0:
  13.0 302.2 all-reduce.2
  317.7 1369.3 all-gather.1
where the time goes:
time: 1700 us
  waiting for transfers between devices  1640 us (96%)
  starting transfers between devices  20.9 us (1%)
    all_gather x1, waiting for transfers between devices, shards(): lax.all_gather(down_rows, ('hst', 'dev'), axis=0, tiled=True)  1370 us
    unnamed x3, waiting for transfers between devices  257 us
  transfers between devices with their start and end apart: 4, of which 3 were waited for; matrix products, arithmetic and copies ran while one was open for 1% of the time, Pallas kernels for 0%

commit v1 on v0

v1 whole, which is shorter than its diff:
```python
import functools

import jax
import jax.numpy as jnp
from jax import lax
from jax.experimental import pallas as pl
from jax.experimental.pallas import tpu as pltpu
from jax.sharding import PartitionSpec as P

CKR = 256
F32 = jnp.float32
BF16 = jnp.bfloat16
VMEM = pl.BlockSpec(memory_space=pltpu.VMEM)
SMEM = pl.BlockSpec(memory_space=pltpu.SMEM)
LIMIT = 40 * 1024 * 1024


def gelu_value(inputs):
    cubic = inputs * inputs * inputs
    tangent = jnp.tanh(0.7978845608 * (inputs + 0.044715 * cubic))
    return 0.5 * inputs * (1.0 + tangent)


def gelu_slope(inputs):
    squared = inputs * inputs
    tangent = jnp.tanh(0.7978845608 * (inputs + 0.044715 * squared * inputs))
    return 0.5 * (1.0 + tangent) + 0.5 * inputs * (1.0 - tangent * tangent) * 0.7978845608 * (
        1.0 + 3.0 * 0.044715 * squared
    )


def lane_group(shape):
    return lax.broadcasted_iota(jnp.int32, shape, 1) // 32


def first_kernel(start_ref, states_ref, rows_ref, out_ref):
    start = pl.multiple_of(start_ref[0, 0], 8)
    rows = jnp.concatenate([rows_ref[...].astype(F32), jnp.zeros((24, 64), F32)], axis=1)
    group = lane_group((8, 128))
    packed = []
    for c in range(2):
        total = jnp.zeros((8, 128), F32)
        for g in range(3):
            moved = pltpu.roll(rows[8 * g : 8 * g + 8], (32 * (g - c)) % 128, 1)
            total = jnp.where(group == g, moved, total)
        packed.append(total)
    blank = jnp.zeros((4, 128), F32)
    for pair in range(32):
        tiles = []
        for i in range(3):
            tile = 3 * pair + i
            tiles.append(states_ref[tile // 32, pl.ds(start + tile % 32 * 8, 8), :])
        flat = jnp.concatenate(tiles, axis=0)
        for half in range(2):
            out_ref[2 * pair + half] = jnp.concatenate(
                [flat[12 * half : 12 * half + 12], packed[half], blank], axis=0
            ).astype(BF16)


def weight_kernel(got_ref, out_ref):
    group = lane_group((8, 128))

    def body(p, carry):
        out = [jnp.zeros((8, 128), F32)] * 3
        for q in range(4):
            piece = got_ref[q * 16 + p].astype(F32)[12:20]
            for g in range(3):
                moved = pltpu.roll(piece, (32 * (q - g)) % 128, 1)
                out[g] = jnp.where(group == q, moved, out[g])
        out_ref[p] = jnp.concatenate(out, axis=0).astype(BF16)
        return carry

    lax.fori_loop(0, 16, body, 0)


def second_kernel(inverse_ref, got_ref, sum_ref, other_ref, out_ref):
    group = lane_group((8, 128))

    def body(p, carry):
        total = sum_ref[p] + other_ref[p].astype(F32) * 4.0
        for q in range(4):
            packed = jnp.zeros((8, 128), F32)
            for g in range(3):
                moved = pltpu.roll(total[8 * g : 8 * g + 8], (32 * (g - q)) % 128, 1)
                packed = jnp.where(group == g, moved, packed)
            high = packed.astype(BF16).astype(F32)
            t = q * 16 + p
            first = got_ref[inverse_ref[0, t]].astype(F32)[:12]
            second = got_ref[inverse_ref[1, t]].astype(F32)[:12]
            out_ref[t] = jnp.concatenate([first, second, high, packed - high], axis=0).astype(BF16)
        return carry

    lax.fori_loop(0, 16, body, 0)


def last_kernel(scale, got_ref, backup_ref, grad_ref):
    totals = [jnp.zeros((8, 128), F32)] * 2
    for pair in range(32):
        blocks = [got_ref[2 * pair].astype(F32), got_ref[2 * pair + 1].astype(F32)]
        for c in range(2):
            totals[c] = totals[c] + (blocks[c][24:32] + blocks[c][32:40])
        for k in range(2):
            flat = jnp.concatenate([block[12 * k : 12 * k + 12] for block in blocks], axis=0)
            for i in range(3):
                tile = 3 * pair + i
                backup_ref[tile // 32, k, pl.ds(tile % 32 * 8, 8), :] = flat[8 * i : 8 * i + 8]
    group = lane_group((8, 128))
    for g in range(3):
        low = pltpu.roll(totals[0], (-32 * g) % 128, 1)
        high = pltpu.roll(totals[1], (32 - 32 * g) % 128, 1)
        grad_ref[pl.ds(8 * g, 8), :] = (jnp.where(group == 0, low, high) * scale)[:, :64]


def term_kernel(core_ref, pre_ref, g0, g1, g2, g3, own_ref, other_ref, right_ref):
    @pl.when(pl.program_id(0) == 0)
    def _():
        act = gelu_value(pre_ref[...].astype(F32))
        low = jnp.concatenate([act, jnp.zeros((128, 192), F32)], axis=1)
        lane = lax.broadcasted_iota(jnp.int32, (128, 256), 1)
        mine = core_ref[0]
        for q in range(4):
            a = pltpu.roll(low, 32 * q, 1)
            b = pltpu.roll(low, (32 * q - 32) % 256, 1)
            keep, send = jnp.where(mine == 0, a, b), jnp.where(mine == 0, b, a)
            send = pltpu.roll(send, 128, 1)
            both = jnp.where(
                lane // 32 == q, keep, jnp.where(lane // 32 == q + 4, send, 0.0)
            )
            right_ref[q] = both.astype(BF16)

    total = None
    for q, g in enumerate((g0, g1, g2, g3)):
        part = lax.dot_general(
            g[...], right_ref[q], (((0,), (0,)), ((), ())), preferred_element_type=F32
        )
        total = part if total is None else total + part
    for p in range(2):
        for yh in range(2):
            for x in range(4):
                at = ((p * 2 + yh) * 4 + x) * 24
                own_ref[x, yh, p] = total[at : at + 24, :128]
                other_ref[x, yh, p] = total[at : at + 24, 128:]


def back_kernel(place_ref, own_ref, other_ref, pre_ref, g0, g1, g2, g3, out_ref, weight_ref, acc_ref):
    step = pl.program_id(0)

    @pl.when(step == 0)
    def _():
        acc_ref[...] = jnp.zeros_like(acc_ref)

    mine = place_ref[1]
    for p in range(2):
        for yh in range(2):
            for x in range(4):
                at = ((p * 2 + yh) * 4 + x) * 24
                k = x ^ mine
                weight_ref[pl.ds(at, 24), :128] = own_ref[k, yh, p].astype(F32)
                weight_ref[pl.ds(at, 24), 128:] = other_ref[k, yh, p].astype(F32)
    weight = weight_ref[...].astype(BF16)
    for q, g in enumerate((g0, g1, g2, g3)):
        acc_ref[q] += jnp.dot(g[...], weight, preferred_element_type=F32)

    @pl.when(step == pl.num_programs(0) - 1)
    def _():
        lane = lax.broadcasted_iota(jnp.int32, (128, 256), 1)
        total = jnp.zeros((128, 256), F32)
        for q in range(4):
            total = jnp.where(lane // 32 % 4 == q, acc_ref[q], total)
        halves = []
        for c in range(2):
            half = total[:, 128 * c : 128 * c + 128]
            half = half + pltpu.roll(half, 64, 1)
            halves.append(half + pltpu.roll(half, 32, 1))
        is_low = lax.broadcasted_iota(jnp.int32, (128, 128), 1) // 32 % 2 == place_ref[0]
        both = jnp.where(is_low, halves[0], halves[1])[:, :64]
        out_ref[...] = (both * gelu_slope(pre_ref[...].astype(F32))).astype(BF16)


def call(kernel, out_shape, in_specs, **kwargs):
    return pl.pallas_call(
        kernel,
        out_shape=out_shape,
        in_specs=in_specs,
        out_specs=jax.tree.map(lambda _: VMEM, out_shape),
        compiler_params=pltpu.CompilerParams(vmem_limit_bytes=LIMIT),
        **kwargs,
    )


def grad_specs():
    return [pl.BlockSpec((128, 384), lambda s, c, q=q: (0, q * 8 + s)) for q in range(4)]


def shards(grad_out, pre_act, down_rows, states, partner_hosts, slice_start):
    axes = ("hst", "dev")
    core = lax.axis_index("hst") % 2
    x = lax.axis_index("dev") % 4
    yh = lax.axis_index("dev") // 4

    def flip(array, bits):
        return lax.ppermute(array, axes, [(i, i ^ bits) for i in range(512)])

    shape = jax.ShapeDtypeStruct
    send1 = call(first_kernel, shape((64, 24, 128), BF16), [SMEM, VMEM, VMEM])(
        slice_start, states, down_rows
    )
    got1 = lax.all_to_all(send1, "hst", 0, 0, tiled=True)

    blocks = pl.BlockSpec((4, 2, 2, 24, 128), lambda s, c: (0, 0, s, 0, 0))
    fixed = pl.BlockSpec((128, 64), lambda s, c: (0, 0))
    keep, send = pl.pallas_call(
        term_kernel,
        out_shape=[shape((4, 2, 16, 24, 128), F32)] * 2,
        grid_spec=pltpu.PrefetchScalarGridSpec(
            num_scalar_prefetch=1,
            grid=(8,),
            in_specs=[fixed] + grad_specs(),
            out_specs=[blocks, blocks],
            scratch_shapes=[pltpu.VMEM((4, 128, 256), BF16)],
        ),
        compiler_params=pltpu.CompilerParams(vmem_limit_bytes=LIMIT),
    )(core[None], pre_act, *[grad_out] * 4)
    arrived = flip(send, 8)

    def pick(k):
        return keep[x ^ k] + arrived[x ^ k]

    parts = [flip(pick(k).astype(jnp.float16), k) for k in (1, 2, 3)]
    summed = pick(0)
    for part in parts:
        summed = summed + part.astype(F32)
    mine = summed[yh]
    other = flip((summed[1 - yh] * 0.25).astype(jnp.float16), 4)

    sources = jnp.arange(64, dtype=jnp.int32)
    matches = partner_hosts[:, :, None] == sources[None, None, :]
    inverse = jnp.sum(jnp.where(matches, sources[:, None, None], 0), axis=0)
    send2 = call(second_kernel, shape((64, 40, 128), BF16), [SMEM, VMEM, VMEM, VMEM])(
        inverse, got1, mine, other.astype(F32)
    )
    got2 = lax.all_to_all(send2, "hst", 0, 0, tiled=True)
    backup, grad_bucket = call(
        functools.partial(last_kernel, 1.0 / 512),
        [shape((3, 2, CKR, 128), F32), shape((24, 64), F32)],
        [VMEM],
    )(got2)

    held = call(weight_kernel, shape((16, 24, 128), BF16), [VMEM])(got1)
    across = flip(held, 4)
    pair = jnp.where(yh == 0, jnp.stack([held, across]), jnp.stack([across, held]))
    own = jnp.stack([pair] + [flip(pair, k) for k in (1, 2, 3)])
    far = flip(own, 8)
    wide = pl.BlockSpec((4, 2, 2, 24, 128), lambda s, c: (0, 0, s, 0, 0))
    grad_pre = pl.pallas_call(
        back_kernel,
        out_shape=shape((128, 64), BF16),
        grid_spec=pltpu.PrefetchScalarGridSpec(
            num_scalar_prefetch=1,
            grid=(8,),
            in_specs=[wide, wide, fixed] + grad_specs(),
            out_specs=fixed,
            scratch_shapes=[pltpu.VMEM((384, 256), F32), pltpu.VMEM((4, 128, 256), F32)],
        ),
        compiler_params=pltpu.CompilerParams(vmem_limit_bytes=LIMIT),
    )(jnp.stack([core, x]), own, far, pre_act, *[grad_out] * 4)
    return (grad_bucket, grad_pre, backup)


def solution(mesh):
    return jax.shard_map(
        shards,
        mesh=mesh,
        in_specs=(
            P(("hst", "dev"), None),
            P(("hst", "dev"), None),
            P(("hst", "dev"), None),
            P(None, ("hst", "dev"), None),
            P(),
            P("hst", "dev"),
        ),
        out_specs=(
            P(("hst", "dev"), None),
            P(("hst", "dev"), None),
            P(None, None, ("hst", "dev"), None),
        ),
        check_vma=False,
    )
```

time: 1700 us -> 105 us (0.06)
  waiting for transfers between devices: 1640 us -> 20 us
  starting transfers between devices: 20.9 us -> 58.6 us
    all_gather x1 -> x0, waiting for transfers between devices: 1370 us -> none  [shards(): lax.all_gather(down_rows, ('hst', 'dev'), axis=0, tiled=True)]
    unnamed x3 -> x0, waiting for transfers between devices: 257 us -> none
    ppermute x0 -> x10, starting transfers between devices: none -> 39.4 us  [flip(): return lax.ppermute(array, axes, [(i, i ^ bits) for i in range(512)])]
  transfers between devices with their start and end apart: 4 -> 12, of which waited for: 3 -> 5; matrix products, arithmetic and copies ran while one was open for 1% -> 5% of each run, Pallas kernels for 0% -> 8%
where the time goes in v1:
time: 105 us; the launch traced here: 104 us
  starting transfers between devices  58.6 us (56%)
  waiting for transfers between devices  20 us (19%)
  Pallas kernels  15 us (14%)
  other arithmetic  4.94 us (5%)
  local copies, waits for them, and re-layouts  4.27 us (4%)
  between operations  1.63 us (2%)
    ppermute x10, starting transfers between devices, flip(): return lax.ppermute(array, axes, [(i, i ^ bits) for i in range(512)])  39.4 us
    ppermute x10, waiting for transfers between devices, flip(): return lax.ppermute(array, axes, [(i, i ^ bits) for i in range(512)])  15 us
    all_to_all x1, starting transfers between devices, shards(): got2 = lax.all_to_all(send2, 'hst', 0, 0, tiled=True)  10.5 us
    all_to_all x1, starting transfers between devices, shards(): got1 = lax.all_to_all(send1, 'hst', 0, 0, tiled=True)  8.65 us
    all_to_all x1, waiting for transfers between devices, shards(): got1 = lax.all_to_all(send1, 'hst', 0, 0, tiled=True)  5.05 us
    unnamed x18, local copies, waits for them, and re-layouts  4.27 us
    pallas_call x1, Pallas kernels, shards(): pl.pallas_call(term_kernel, out_shape=[shape((4, 2, 16, 24, 128), F32)] *...  4.18 us
    pallas_call x1, Pallas kernels, shards(): pl.pallas_call(back_kernel, out_shape=shape((128, 64), BF16), grid_spec=p...  4.06 us
  transfers between devices with their start and end apart: 12, of which 5 were waited for; matrix products, arithmetic and copies ran while one was open for 5% of the time, Pallas kernels for 8%

profile of v1, /device:TPU:1, one launch (start us, length us, event | category | flops | bytes accessed | tf_op | source)
XLA Modules:
  0.0 104.4 jit_solution(3778529617651897843)
XLA Ops:
  1.5 1.9 %copy-done = bf16[128,12288]{1,0:T(8,128)(2,1)S(1)} copy-done((bf16[128,12288]{1,0:T(8,128)(2,1)S(1)}, bf16[128,12288]{1,0:T(8,128)(2,1)}, u32[]{:S(2)}) %copy-start) | copy-done | bytes 3145752
  3.4 4.2 %shard_map.86 = (f32[4,2,16,24,128]{4,3,2,1,0:T(8,128)S(1)}, f32[4,2,16,24,128]{4,3,2,1,0:T(8,128)S(1)}) custom-call(s32[1]{0:T(128)} %bitcast.core_ref, bf16[128,64]{1,0:T(8,128)(2,1)S(1)} %copy.13.pre_ref, bf16[128,12288]{1,0:T(8,128)(2,1)S(1)} %copy-done, bf16[128,12288]{1,0:T(8,128)(2,1)S(1)} %copy-done, bf16[128,12288]{1,0:T(8,128)(2,1)S(1)} %copy-done, ...), custom_call_target="tpu_custom_call" | custom-call | tf_op jit(solution)/shard_map/pallas_call | solution.py:212
  7.6 8.8 %collective-permute-start = (f32[4,2,16,24,128]{4,3,2,1,0:T(8,128)S(1)}, f32[4,2,16,24,128]{4,3,2,1,0:T(8,128)}, u32[]{:S(2)}, u32[]{:S(2)}) collective-permute-start(f32[4,2,16,24,128]{4,3,2,1,0:T(8,128)S(1)} %get-tuple-element.8), channel_id=1, source_target_pairs={{0,8},{1,9},{2,10},{3,11},{4,12},{5,13},{6,14},{7,15},{8,0},{9,1},... | collective-permute-start | bytes 4718600 | tf_op jit(solution)/shard_map/ppermute | solution.py:202
  17.9 8.6 %all-to-all-start = ((bf16[64,24,128]{2,1,0:T(8,128)(2,1)}), bf16[64,24,128]{2,1,0:T(8,128)(2,1)S(1)}, u32[]{:S(2)}, u32[]{:S(2)}) async-start(bf16[64,24,128]{2,1,0:T(8,128)(2,1)} %shard_map.85), calls=%async_computation | async-start | bytes 786432 | tf_op jit(solution)/shard_map/all_to_all | solution.py:208
  26.6 1.4 %fusion.2 = (f16[2,16,24,128]{3,2,1,0:T(8,128)(2,1)S(1)}, f16[2,16,24,128]{3,2,1,0:T(8,128)(2,1)S(1)}, f16[2,16,24,128]{3,2,1,0:T(8,128)(2,1)S(1)}) fusion(f32[4,2,16,24,128]{4,3,2,1,0:T(8,128)} %collective-permute-done, s32[]{:T(128)S(6)} %select_n.64, f32[4,2,16,24,128]{4,3,2,1,0:T(8,128)S(1)} %get-tuple-element.7, s32[]{:T(128)S(6)} %select_n.66, ...), kind=kLoop, calls=%fused_computation.7 | loop fusion | flops 589824 | bytes 2949132 | tf_op jit(solution)/shard_map/convert_element_type | solution.py:229
  28.0 3.1 %collective-permute-start.1 = (f16[2,16,24,128]{3,2,1,0:T(8,128)(2,1)S(1)}, f16[2,16,24,128]{3,2,1,0:T(8,128)(2,1)S(1)}, u32[]{:S(2)}, u32[]{:S(2)}) collective-permute-start(f16[2,16,24,128]{3,2,1,0:T(8,128)(2,1)S(1)} %get-tuple-element.17), channel_id=1, source_target_pairs={{0,1},{1,0},{2,3},{3,2},{4,5},{5,4},{6,7},{7,6},{8,9},{9,8},{10,11... | collective-permute-start | bytes 589832 | tf_op jit(solution)/shard_map/ppermute | solution.py:202
  31.1 4.4 %collective-permute-start.2 = (f16[2,16,24,128]{3,2,1,0:T(8,128)(2,1)S(1)}, f16[2,16,24,128]{3,2,1,0:T(8,128)(2,1)S(1)}, u32[]{:S(2)}, u32[]{:S(2)}) collective-permute-start(f16[2,16,24,128]{3,2,1,0:T(8,128)(2,1)S(1)} %get-tuple-element.19), channel_id=1, source_target_pairs={{0,2},{1,3},{2,0},{3,1},{4,6},{5,7},{6,4},{7,5},{8,10},{9,11},{10,... | collective-permute-start | bytes 589832 | tf_op jit(solution)/shard_map/ppermute | solution.py:202
  35.5 2.1 %collective-permute-start.3 = (f16[2,16,24,128]{3,2,1,0:T(8,128)(2,1)S(1)}, f16[2,16,24,128]{3,2,1,0:T(8,128)(2,1)S(1)}, u32[]{:S(2)}, u32[]{:S(2)}) collective-permute-start(f16[2,16,24,128]{3,2,1,0:T(8,128)(2,1)S(1)} %get-tuple-element.18), channel_id=1, source_target_pairs={{0,3},{1,2},{2,1},{3,0},{4,7},{5,6},{6,5},{7,4},{8,11},{9,10},{10,... | collective-permute-start | bytes 589832 | tf_op jit(solution)/shard_map/ppermute | solution.py:202
  37.6 5.0 %all-to-all-done.got_ref = bf16[64,24,128]{2,1,0:T(8,128)(2,1)S(1)} async-done(((bf16[64,24,128]{2,1,0:T(8,128)(2,1)}), bf16[64,24,128]{2,1,0:T(8,128)(2,1)S(1)}, u32[]{:S(2)}, u32[]{:S(2)}) %all-to-all-start) | async-done | bytes 393248 | tf_op jit(solution)/shard_map/all_to_all | solution.py:208
  42.7 1.9 %shard_map.89 = bf16[16,24,128]{2,1,0:T(8,128)(2,1)} custom-call(bf16[64,24,128]{2,1,0:T(8,128)(2,1)S(1)} %all-to-all-done.got_ref), custom_call_target="tpu_custom_call" | custom-call | tf_op jit(solution)/shard_map/pallas_call | solution.py:249
  44.6 4.7 %collective-permute-start.5 = (bf16[16,24,128]{2,1,0:T(8,128)(2,1)}, bf16[16,24,128]{2,1,0:T(8,128)(2,1)}, u32[]{:S(2)}, u32[]{:S(2)}) collective-permute-start(bf16[16,24,128]{2,1,0:T(8,128)(2,1)} %shard_map.89), channel_id=1, source_target_pairs={{0,4},{1,5},{2,6},{3,7},{4,0},{5,1},{6,2},{7,3},{8,12},{9,13},{10,... | collective-permute-start | bytes 294920 | tf_op jit(solution)/shard_map/ppermute | solution.py:202
  50.5 4.4 %collective-permute-start.4 = (f16[16,24,128]{2,1,0:T(8,128)(2,1)S(1)}, f16[16,24,128]{2,1,0:T(8,128)(2,1)S(1)}, u32[]{:S(2)}, u32[]{:S(2)}) collective-permute-start(f16[16,24,128]{2,1,0:T(8,128)(2,1)S(1)} %get-tuple-element.20), channel_id=1, source_target_pairs={{0,4},{1,5},{2,6},{3,7},{4,0},{5,1},{6,2},{7,3},{8,12},{9,13},{10,... | collective-permute-start | bytes 294920 | tf_op jit(solution)/shard_map/ppermute | solution.py:202
  55.1 6.7 %collective-permute-done.4 = f16[16,24,128]{2,1,0:T(8,128)(2,1)S(1)} collective-permute-done((f16[16,24,128]{2,1,0:T(8,128)(2,1)S(1)}, f16[16,24,128]{2,1,0:T(8,128)(2,1)S(1)}, u32[]{:S(2)}, u32[]{:S(2)}) %collective-permute-start.4) | collective-permute-done | bytes 98336 | tf_op jit(solution)/shard_map/ppermute | solution.py:202
  61.8 1.9 %shard_map.87 = bf16[64,40,128]{2,1,0:T(8,128)(2,1)S(1)} custom-call(s32[2,64]{1,0:T(2,128)S(1)} %select_reduce_fusion.inverse_ref, bf16[64,24,128]{2,1,0:T(8,128)(2,1)S(1)} %all-to-all-done.got_ref, f32[16,24,128]{2,1,0:T(8,128)S(1)} %get-tuple-element.21.sum_ref, f32[16,24,128]{2,1,0:T(8,128)S(1)} %convert_element_type.47.other_ref), custom_call_target="tpu_custom_call" | custom-call | tf_op jit(solution)/shard_map/pallas_call | solution.py:239
  64.5 10.5 %all-to-all-start.1 = ((bf16[64,40,128]{2,1,0:T(8,128)(2,1)}), bf16[64,40,128]{2,1,0:T(8,128)(2,1)}, u32[]{:S(2)}, u32[]{:S(2)}) async-start(bf16[64,40,128]{2,1,0:T(8,128)(2,1)} %copy-done.2), calls=%async_computation.1 | async-start | bytes 1310720 | tf_op jit(solution)/shard_map/all_to_all | solution.py:242
  76.1 1.9 %collective-permute-start.6 = (bf16[2,16,24,128]{3,2,1,0:T(8,128)(2,1)S(1)}, bf16[2,16,24,128]{3,2,1,0:T(8,128)(2,1)S(1)}, u32[]{:S(2)}, u32[]{:S(2)}) collective-permute-start(bf16[2,16,24,128]{3,2,1,0:T(8,128)(2,1)S(1)} %maximum_select_fusion.1), channel_id=1, source_target_pairs={{0,1},{1,0},{2,3},{3,2},{4,5},{5,4},{6,7},{7,6},{8,9},{9,8},{10,11... | collective-permute-start | bytes 589832 | tf_op jit(solution)/shard_map/ppermute | solution.py:202
  78.1 3.3 %collective-permute-start.7 = (bf16[2,16,24,128]{3,2,1,0:T(8,128)(2,1)S(1)}, bf16[2,16,24,128]{3,2,1,0:T(8,128)(2,1)S(1)}, u32[]{:S(2)}, u32[]{:S(2)}) collective-permute-start(bf16[2,16,24,128]{3,2,1,0:T(8,128)(2,1)S(1)} %maximum_select_fusion.1), channel_id=1, source_target_pairs={{0,2},{1,3},{2,0},{3,1},{4,6},{5,7},{6,4},{7,5},{8,10},{9,11},{10,... | collective-permute-start | bytes 589832 | tf_op jit(solution)/shard_map/ppermute | solution.py:202
  81.4 4.4 %collective-permute-start.8 = (bf16[2,16,24,128]{3,2,1,0:T(8,128)(2,1)S(1)}, bf16[2,16,24,128]{3,2,1,0:T(8,128)(2,1)S(1)}, u32[]{:S(2)}, u32[]{:S(2)}) collective-permute-start(bf16[2,16,24,128]{3,2,1,0:T(8,128)(2,1)S(1)} %maximum_select_fusion.1), channel_id=1, source_target_pairs={{0,3},{1,2},{2,1},{3,0},{4,7},{5,6},{6,5},{7,4},{8,11},{9,10},{10,... | collective-permute-start | bytes 589832 | tf_op jit(solution)/shard_map/ppermute | solution.py:202
  86.8 1.7 %collective-permute-done.7 = bf16[2,16,24,128]{3,2,1,0:T(8,128)(2,1)S(1)} collective-permute-done((bf16[2,16,24,128]{3,2,1,0:T(8,128)(2,1)S(1)}, bf16[2,16,24,128]{3,2,1,0:T(8,128)(2,1)S(1)}, u32[]{:S(2)}, u32[]{:S(2)}) %collective-permute-start.7) | collective-permute-done | bytes 196640 | tf_op jit(solution)/shard_map/ppermute | solution.py:202
  88.6 4.7 %collective-permute-done.8 = bf16[2,16,24,128]{3,2,1,0:T(8,128)(2,1)S(1)} collective-permute-done((bf16[2,16,24,128]{3,2,1,0:T(8,128)(2,1)S(1)}, bf16[2,16,24,128]{3,2,1,0:T(8,128)(2,1)S(1)}, u32[]{:S(2)}, u32[]{:S(2)}) %collective-permute-start.8) | collective-permute-done | bytes 196640 | tf_op jit(solution)/shard_map/ppermute | solution.py:202
  93.4 2.3 %collective-permute-start.9 = (bf16[4,2,16,24,128]{4,3,2,1,0:T(8,128)(2,1)S(1)}, bf16[4,2,16,24,128]{4,3,2,1,0:T(8,128)(2,1)S(1)}, u32[]{:S(2)}, u32[]{:S(2)}) collective-permute-start(bf16[4,2,16,24,128]{4,3,2,1,0:T(8,128)(2,1)S(1)} %pad_maximum_fusion.own_ref), channel_id=1, source_target_pairs={{0,8},{1,9},{2,10},{3,11},{4,12},{5,13},{6,14},{7,15},{8,0},{9,1},... | collective-permute-start | bytes 2359304 | tf_op jit(solution)/shard_map/ppermute | solution.py:202
  95.8 1.8 %collective-permute-done.9.other_ref = bf16[4,2,16,24,128]{4,3,2,1,0:T(8,128)(2,1)S(1)} collective-permute-done((bf16[4,2,16,24,128]{4,3,2,1,0:T(8,128)(2,1)S(1)}, bf16[4,2,16,24,128]{4,3,2,1,0:T(8,128)(2,1)S(1)}, u32[]{:S(2)}, u32[]{:S(2)}) %collective-permute-start.9) | collective-permute-done | bytes 786464 | tf_op jit(solution)/shard_map/ppermute | solution.py:202
  97.6 4.1 %shard_map.90 = bf16[128,64]{1,0:T(8,128)(2,1)S(1)} custom-call(s32[2]{0:T(128)S(1)} %pad_add_fusion.place_ref, bf16[4,2,16,24,128]{4,3,2,1,0:T(8,128)(2,1)S(1)} %pad_maximum_fusion.own_ref, bf16[4,2,16,24,128]{4,3,2,1,0:T(8,128)(2,1)S(1)} %collective-permute-done.9.other_ref, bf16[128,64]{1,0:T(8,128)(2,1)S(1)} %copy-done.5, ...), custom_call_target="tpu_custom_call" | custom-call | tf_op jit(solution)/shard_map/pallas_call | solution.py:255
  102.4 2.1 %shard_map.88 = (f32[3,2,256,128]{3,2,1,0:T(8,128)}, f32[24,64]{1,0:T(8,128)}) custom-call(bf16[64,40,128]{2,1,0:T(8,128)(2,1)} %all-to-all-done.1.got_ref), custom_call_target="tpu_custom_call" | custom-call | tf_op jit(solution)/shard_map/pallas_call | solution.py:243
  (33 shorter events, 6.8 us)
Async XLA Ops:
  1.5 6.1 %copy-start.4 = (bf16[128,64]{1,0:T(8,128)(2,1)}, bf16[128,64]{1,0:T(8,128)(2,1)S(1)}, u32[]{:S(2)}) copy-start(bf16[128,64]{1,0:T(8,128)(2,1)S(1)} %copy.13.pre_ref) | copy-start | bytes 49156
  1.5 1.9 %copy-start = (bf16[128,12288]{1,0:T(8,128)(2,1)S(1)}, bf16[128,12288]{1,0:T(8,128)(2,1)}, u32[]{:S(2)}) copy-start(bf16[128,12288]{1,0:T(8,128)(2,1)} %g3.3) | copy-start | bytes 9437188
  3.4 13.7 %copy-start.3 = (f32[3,320,128]{2,1,0:T(8,128)S(1)}, f32[3,320,128]{2,1,0:T(8,128)}, u32[]{:S(2)}) copy-start(f32[3,320,128]{2,1,0:T(8,128)} %states_ref.1) | copy-start | bytes 1474564
  3.4 13.7 %copy-start.6 = (bf16[24,64]{1,0:T(8,128)(2,1)S(1)}, bf16[24,64]{1,0:T(8,128)(2,1)}, u32[]{:S(2)}) copy-start(bf16[24,64]{1,0:T(8,128)(2,1)} %rows_ref.1) | copy-start | bytes 9220
  7.6 19.0 %collective-permute-start = (f32[4,2,16,24,128]{4,3,2,1,0:T(8,128)S(1)}, f32[4,2,16,24,128]{4,3,2,1,0:T(8,128)}, u32[]{:S(2)}, u32[]{:S(2)}) collective-permute-start(f32[4,2,16,24,128]{4,3,2,1,0:T(8,128)S(1)} %get-tuple-element.8), channel_id=1, source_target_pairs={{0,8},{1,9},{2,10},{3,11},{4,12},{5,13},{6,14},{7,15},{8,0},{9,1},... | collective-permute-start | bytes 4718600 | tf_op jit(solution)/shard_map/ppermute | solution.py:202
  17.9 24.8 %all-to-all-start = ((bf16[64,24,128]{2,1,0:T(8,128)(2,1)}), bf16[64,24,128]{2,1,0:T(8,128)(2,1)S(1)}, u32[]{:S(2)}, u32[]{:S(2)}) async-start(bf16[64,24,128]{2,1,0:T(8,128)(2,1)} %shard_map.85), calls=%async_computation | async-start | bytes 786432 | tf_op jit(solution)/shard_map/all_to_all | solution.py:208
  28.0 27.0 %copy-start.7 = (s32[64,2]{0,1:T(2,128)S(1)}, s32[64,2]{0,1:T(2,128)}, u32[]{:S(2)}) copy-start(s32[64,2]{0,1:T(2,128)} %param.10) | copy-start | bytes 1540
  28.0 21.4 %collective-permute-start.1 = (f16[2,16,24,128]{3,2,1,0:T(8,128)(2,1)S(1)}, f16[2,16,24,128]{3,2,1,0:T(8,128)(2,1)S(1)}, u32[]{:S(2)}, u32[]{:S(2)}) collective-permute-start(f16[2,16,24,128]{3,2,1,0:T(8,128)(2,1)S(1)} %get-tuple-element.17), channel_id=1, source_target_pairs={{0,1},{1,0},{2,3},{3,2},{4,5},{5,4},{6,7},{7,6},{8,9},{9,8},{10,11... | collective-permute-start | bytes 589832 | tf_op jit(solution)/shard_map/ppermute | solution.py:202
  31.1 18.3 %collective-permute-start.2 = (f16[2,16,24,128]{3,2,1,0:T(8,128)(2,1)S(1)}, f16[2,16,24,128]{3,2,1,0:T(8,128)(2,1)S(1)}, u32[]{:S(2)}, u32[]{:S(2)}) collective-permute-start(f16[2,16,24,128]{3,2,1,0:T(8,128)(2,1)S(1)} %get-tuple-element.19), channel_id=1, source_target_pairs={{0,2},{1,3},{2,0},{3,1},{4,6},{5,7},{6,4},{7,5},{8,10},{9,11},{10,... | collective-permute-start | bytes 589832 | tf_op jit(solution)/shard_map/ppermute | solution.py:202
  35.5 13.9 %collective-permute-start.3 = (f16[2,16,24,128]{3,2,1,0:T(8,128)(2,1)S(1)}, f16[2,16,24,128]{3,2,1,0:T(8,128)(2,1)S(1)}, u32[]{:S(2)}, u32[]{:S(2)}) collective-permute-start(f16[2,16,24,128]{3,2,1,0:T(8,128)(2,1)S(1)} %get-tuple-element.18), channel_id=1, source_target_pairs={{0,3},{1,2},{2,1},{3,0},{4,7},{5,6},{6,5},{7,4},{8,11},{9,10},{10,... | collective-permute-start | bytes 589832 | tf_op jit(solution)/shard_map/ppermute | solution.py:202
  44.6 30.5 %collective-permute-start.5 = (bf16[16,24,128]{2,1,0:T(8,128)(2,1)}, bf16[16,24,128]{2,1,0:T(8,128)(2,1)}, u32[]{:S(2)}, u32[]{:S(2)}) collective-permute-start(bf16[16,24,128]{2,1,0:T(8,128)(2,1)} %shard_map.89), channel_id=1, source_target_pairs={{0,4},{1,5},{2,6},{3,7},{4,0},{5,1},{6,2},{7,3},{8,12},{9,13},{10,... | collective-permute-start | bytes 294920 | tf_op jit(solution)/shard_map/ppermute | solution.py:202
  50.5 11.2 %collective-permute-start.4 = (f16[16,24,128]{2,1,0:T(8,128)(2,1)S(1)}, f16[16,24,128]{2,1,0:T(8,128)(2,1)S(1)}, u32[]{:S(2)}, u32[]{:S(2)}) collective-permute-start(f16[16,24,128]{2,1,0:T(8,128)(2,1)S(1)} %get-tuple-element.20), channel_id=1, source_target_pairs={{0,4},{1,5},{2,6},{3,7},{4,0},{5,1},{6,2},{7,3},{8,12},{9,13},{10,... | collective-permute-start | bytes 294920 | tf_op jit(solution)/shard_map/ppermute | solution.py:202
  63.7 0.8 copy-start.2
  64.5 33.1 %copy-start.1 = (bf16[128,12288]{1,0:T(8,128)(2,1)S(1)}, bf16[128,12288]{1,0:T(8,128)(2,1)}, u32[]{:S(2)}) copy-start(bf16[128,12288]{1,0:T(8,128)(2,1)} %g3.3) | copy-start | bytes 9437188
  64.5 33.1 %copy-start.5 = (bf16[128,64]{1,0:T(8,128)(2,1)S(1)}, bf16[128,64]{1,0:T(8,128)(2,1)}, u32[]{:S(2)}) copy-start(bf16[128,64]{1,0:T(8,128)(2,1)} %copy-done.4) | copy-start | bytes 49156
  64.5 37.8 %all-to-all-start.1 = ((bf16[64,40,128]{2,1,0:T(8,128)(2,1)}), bf16[64,40,128]{2,1,0:T(8,128)(2,1)}, u32[]{:S(2)}, u32[]{:S(2)}) async-start(bf16[64,40,128]{2,1,0:T(8,128)(2,1)} %copy-done.2), calls=%async_computation.1 | async-start | bytes 1310720 | tf_op jit(solution)/shard_map/all_to_all | solution.py:242
  76.1 10.7 %collective-permute-start.6 = (bf16[2,16,24,128]{3,2,1,0:T(8,128)(2,1)S(1)}, bf16[2,16,24,128]{3,2,1,0:T(8,128)(2,1)S(1)}, u32[]{:S(2)}, u32[]{:S(2)}) collective-permute-start(bf16[2,16,24,128]{3,2,1,0:T(8,128)(2,1)S(1)} %maximum_select_fusion.1), channel_id=1, source_target_pairs={{0,1},{1,0},{2,3},{3,2},{4,5},{5,4},{6,7},{7,6},{8,9},{9,8},{10,11... | collective-permute-start | bytes 589832 | tf_op jit(solution)/shard_map/ppermute | solution.py:202
  78.1 10.5 %collective-permute-start.7 = (bf16[2,16,24,128]{3,2,1,0:T(8,128)(2,1)S(1)}, bf16[2,16,24,128]{3,2,1,0:T(8,128)(2,1)S(1)}, u32[]{:S(2)}, u32[]{:S(2)}) collective-permute-start(bf16[2,16,24,128]{3,2,1,0:T(8,128)(2,1)S(1)} %maximum_select_fusion.1), channel_id=1, source_target_pairs={{0,2},{1,3},{2,0},{3,1},{4,6},{5,7},{6,4},{7,5},{8,10},{9,11},{10,... | collective-permute-start | bytes 589832 | tf_op jit(solution)/shard_map/ppermute | solution.py:202
  81.4 12.0 %collective-permute-start.8 = (bf16[2,16,24,128]{3,2,1,0:T(8,128)(2,1)S(1)}, bf16[2,16,24,128]{3,2,1,0:T(8,128)(2,1)S(1)}, u32[]{:S(2)}, u32[]{:S(2)}) collective-permute-start(bf16[2,16,24,128]{3,2,1,0:T(8,128)(2,1)S(1)} %maximum_select_fusion.1), channel_id=1, source_target_pairs={{0,3},{1,2},{2,1},{3,0},{4,7},{5,6},{6,5},{7,4},{8,11},{9,10},{10,... | collective-permute-start | bytes 589832 | tf_op jit(solution)/shard_map/ppermute | solution.py:202
  93.4 4.2 %collective-permute-start.9 = (bf16[4,2,16,24,128]{4,3,2,1,0:T(8,128)(2,1)S(1)}, bf16[4,2,16,24,128]{4,3,2,1,0:T(8,128)(2,1)S(1)}, u32[]{:S(2)}, u32[]{:S(2)}) collective-permute-start(bf16[4,2,16,24,128]{4,3,2,1,0:T(8,128)(2,1)S(1)} %pad_maximum_fusion.own_ref), channel_id=1, source_target_pairs={{0,8},{1,9},{2,10},{3,11},{4,12},{5,13},{6,14},{7,15},{8,0},{9,1},... | collective-permute-start | bytes 2359304 | tf_op jit(solution)/shard_map/ppermute | solution.py:202

commit v2 on v1

--- a/solution.py
+++ b/solution.py
@@ -59,38 +59,30 @@
 
 def weight_kernel(got_ref, out_ref):
     group = lane_group((8, 128))
-
-    def body(p, carry):
+    for p in range(16):
         out = [jnp.zeros((8, 128), F32)] * 3
         for q in range(4):
             piece = got_ref[q * 16 + p].astype(F32)[12:20]
             for g in range(3):
-                moved = pltpu.roll(piece, (32 * (q - g)) % 128, 1)
+                moved = pltpu.roll(piece, (32 * (q - g)) % 128, 1) if g != q else piece
                 out[g] = jnp.where(group == q, moved, out[g])
         out_ref[p] = jnp.concatenate(out, axis=0).astype(BF16)
-        return carry
-
-    lax.fori_loop(0, 16, body, 0)
 
 
 def second_kernel(inverse_ref, got_ref, sum_ref, other_ref, out_ref):
     group = lane_group((8, 128))
-
-    def body(p, carry):
-        total = sum_ref[p] + other_ref[p].astype(F32) * 4.0
+    for p in range(16):
+        total = sum_ref[p] + other_ref[p] * 4.0
         for q in range(4):
             packed = jnp.zeros((8, 128), F32)
             for g in range(3):
-                moved = pltpu.roll(total[8 * g : 8 * g + 8], (32 * (g - q)) % 128, 1)
+                moved = total[8 * g : 8 * g + 8]
+                if g != q:
+                    moved = pltpu.roll(moved, (32 * (g - q)) % 128, 1)
                 packed = jnp.where(group == g, moved, packed)
-            high = packed.astype(BF16).astype(F32)
             t = q * 16 + p
-            first = got_ref[inverse_ref[0, t]].astype(F32)[:12]
-            second = got_ref[inverse_ref[1, t]].astype(F32)[:12]
-            out_ref[t] = jnp.concatenate([first, second, high, packed - high], axis=0).astype(BF16)
-        return carry
-
-    lax.fori_loop(0, 16, body, 0)
+            rows = [got_ref[inverse_ref[k, t]].astype(F32)[:12] for k in range(2)]
+            out_ref[t] = jnp.concatenate(rows + [packed], axis=0).astype(BF16)
 
 
 def last_kernel(scale, got_ref, backup_ref, grad_ref):
@@ -98,7 +90,7 @@
     for pair in range(32):
         blocks = [got_ref[2 * pair].astype(F32), got_ref[2 * pair + 1].astype(F32)]
         for c in range(2):
-            totals[c] = totals[c] + (blocks[c][24:32] + blocks[c][32:40])
+            totals[c] = totals[c] + blocks[c][24:]
         for k in range(2):
             flat = jnp.concatenate([block[12 * k : 12 * k + 12] for block in blocks], axis=0)
             for i in range(3):
@@ -114,7 +106,7 @@
 def term_kernel(core_ref, pre_ref, g0, g1, g2, g3, own_ref, other_ref, right_ref):
     @pl.when(pl.program_id(0) == 0)
     def _():
-        act = gelu_value(pre_ref[...].astype(F32))
+        act = gelu_value(pre_ref[...].astype(F32)).T
         low = jnp.concatenate([act, jnp.zeros((128, 192), F32)], axis=1)
         lane = lax.broadcasted_iota(jnp.int32, (128, 256), 1)
         mine = core_ref[0]
@@ -149,14 +141,13 @@
     def _():
         acc_ref[...] = jnp.zeros_like(acc_ref)
 
-    mine = place_ref[1]
     for p in range(2):
         for yh in range(2):
+            j = yh ^ place_ref[1]
             for x in range(4):
                 at = ((p * 2 + yh) * 4 + x) * 24
-                k = x ^ mine
-                weight_ref[pl.ds(at, 24), :128] = own_ref[k, yh, p].astype(F32)
-                weight_ref[pl.ds(at, 24), 128:] = other_ref[k, yh, p].astype(F32)
+                weight_ref[pl.ds(at, 24), :128] = own_ref[x, j, p].astype(F32)
+                weight_ref[pl.ds(at, 24), 128:] = other_ref[x, j, p].astype(F32)
     weight = weight_ref[...].astype(BF16)
     for q, g in enumerate((g0, g1, g2, g3)):
         acc_ref[q] += jnp.dot(g[...], weight, preferred_element_type=F32)
@@ -173,7 +164,7 @@
             half = half + pltpu.roll(half, 64, 1)
             halves.append(half + pltpu.roll(half, 32, 1))
         is_low = lax.broadcasted_iota(jnp.int32, (128, 128), 1) // 32 % 2 == place_ref[0]
-        both = jnp.where(is_low, halves[0], halves[1])[:, :64]
+        both = jnp.where(is_low, halves[0], halves[1]).T[:64]
         out_ref[...] = (both * gelu_slope(pre_ref[...].astype(F32))).astype(BF16)
 
 
@@ -208,7 +199,7 @@
     got1 = lax.all_to_all(send1, "hst", 0, 0, tiled=True)
 
     blocks = pl.BlockSpec((4, 2, 2, 24, 128), lambda s, c: (0, 0, s, 0, 0))
-    fixed = pl.BlockSpec((128, 64), lambda s, c: (0, 0))
+    fixed = pl.BlockSpec((64, 128), lambda s, c: (0, 0))
     keep, send = pl.pallas_call(
         term_kernel,
         out_shape=[shape((4, 2, 16, 24, 128), F32)] * 2,
@@ -220,13 +211,15 @@
             scratch_shapes=[pltpu.VMEM((4, 128, 256), BF16)],
         ),
         compiler_params=pltpu.CompilerParams(vmem_limit_bytes=LIMIT),
-    )(core[None], pre_act, *[grad_out] * 4)
+    )(core[None], pre_act.T, *[grad_out] * 4)
     arrived = flip(send, 8)
 
     def pick(k):
         return keep[x ^ k] + arrived[x ^ k]
 
-    parts = [flip(pick(k).astype(jnp.float16), k) for k in (1, 2, 3)]
+    leaving = [pick(k).astype(jnp.float16) for k in (1, 3, 2)]
+    parts = [flip(part, k) for part, k in zip(leaving, (1, 3, 2))]
+    got1, _ = lax.optimization_barrier((got1, parts[0]))
     summed = pick(0)
     for part in parts:
         summed = summed + part.astype(F32)
@@ -236,7 +229,10 @@
     sources = jnp.arange(64, dtype=jnp.int32)
     matches = partner_hosts[:, :, None] == sources[None, None, :]
     inverse = jnp.sum(jnp.where(matches, sources[:, None, None], 0), axis=0)
-    send2 = call(second_kernel, shape((64, 40, 128), BF16), [SMEM, VMEM, VMEM, VMEM])(
+    held = call(weight_kernel, shape((16, 24, 128), BF16), [VMEM])(got1)
+    across = flip(held, 4)
+    inverse, _ = lax.optimization_barrier((inverse, across))
+    send2 = call(second_kernel, shape((64, 32, 128), BF16), [SMEM, VMEM, VMEM, VMEM])(
         inverse, got1, mine, other.astype(F32)
     )
     got2 = lax.all_to_all(send2, "hst", 0, 0, tiled=True)
@@ -246,15 +242,16 @@
         [VMEM],
     )(got2)
 
-    held = call(weight_kernel, shape((16, 24, 128), BF16), [VMEM])(got1)
-    across = flip(held, 4)
-    pair = jnp.where(yh == 0, jnp.stack([held, across]), jnp.stack([across, held]))
-    own = jnp.stack([pair] + [flip(pair, k) for k in (1, 2, 3)])
+    held, across, _ = lax.optimization_barrier((held, across, send2))
+    pair = jnp.concatenate([held, across]).reshape(768, 128)
+    lines = [[0, 1, 2, 3], [4, 5, 6, 7]]
+    own = lax.all_gather(pair, "dev", axis=0, tiled=True, axis_index_groups=lines)
+    own = own.reshape(4, 2, 16, 24, 128)
     far = flip(own, 8)
     wide = pl.BlockSpec((4, 2, 2, 24, 128), lambda s, c: (0, 0, s, 0, 0))
     grad_pre = pl.pallas_call(
         back_kernel,
-        out_shape=shape((128, 64), BF16),
+        out_shape=shape((64, 128), BF16),
         grid_spec=pltpu.PrefetchScalarGridSpec(
             num_scalar_prefetch=1,
             grid=(8,),
@@ -263,8 +260,8 @@
             scratch_shapes=[pltpu.VMEM((384, 256), F32), pltpu.VMEM((4, 128, 256), F32)],
         ),
         compiler_params=pltpu.CompilerParams(vmem_limit_bytes=LIMIT),
-    )(jnp.stack([core, x]), own, far, pre_act, *[grad_out] * 4)
-    return (grad_bucket, grad_pre, backup)
+    )(jnp.stack([core, yh]), own, far, pre_act.T, *[grad_out] * 4)
+    return (grad_bucket, grad_pre.T, backup)
 
 
 def solution(mesh):

time: 105 us -> 104 us (level)
  blocking collectives: 0 us -> 11.7 us
  waiting for transfers between devices: 20 us -> 13.9 us
  starting transfers between devices: 58.6 us -> 54 us
  Pallas kernels: 15 us -> 12.6 us
    all_gather x0 -> x1, blocking collectives: none -> 11.7 us  [shards(): lax.all_gather(pair, 'dev', axis=0, tiled=True, axis_index_groups=lines)]
    ppermute x10 -> x7, starting transfers between devices: 39.4 us -> 31.4 us  [flip(): return lax.ppermute(array, axes, [(i, i ^ bits) for i in range(512)])]
    all_to_all x1, waiting for transfers between devices: 5.05 us -> 0.01 us  [shards(): got1 = lax.all_to_all(send1, 'hst', 0, 0, tiled=True)]
    all_to_all x1, starting transfers between devices: 10.5 us -> 13.9 us  [shards(): got2 = lax.all_to_all(send2, 'hst', 0, 0, tiled=True)]
    select_n x2 -> x0, other arithmetic: 2.15 us -> none  [shards(): jnp.where(yh == 0, jnp.stack([held, across]), jnp.stack([across, held]))]
    pallas_call x1, Pallas kernels: 1.92 us -> 0.16 us  [shards(): held = call(weight_kernel, shape((16, 24, 128), BF16), [VMEM])(got1)]
    ppermute x10 -> x7, waiting for transfers between devices: 15 us -> 13.9 us  [flip(): return lax.ppermute(array, axes, [(i, i ^ bits) for i in range(512)])]
    unnamed x18 -> x22, local copies, waits for them, and re-layouts: 4.27 us -> 4.95 us
  transfers between devices with their start and end apart: 12 -> 9, of which waited for: 5 -> 4; matrix products, arithmetic and copies ran while one was open for 5% -> 4% of each run, Pallas kernels for 8% -> 5%
where the time goes in v2:
time: 104 us; the launch traced here: 103 us
  starting transfers between devices  54 us (52%)
  waiting for transfers between devices  13.9 us (13%)
  Pallas kernels  12.6 us (12%)
  blocking collectives  11.7 us (11%)
  local copies, waits for them, and re-layouts  4.95 us (5%)
  other arithmetic  4.3 us (4%)
  between operations  1.55 us (1%)
    ppermute x7, starting transfers between devices, flip(): return lax.ppermute(array, axes, [(i, i ^ bits) for i in range(512)])  31.4 us
    all_to_all x1, starting transfers between devices, shards(): got2 = lax.all_to_all(send2, 'hst', 0, 0, tiled=True)  13.9 us
    ppermute x7, waiting for transfers between devices, flip(): return lax.ppermute(array, axes, [(i, i ^ bits) for i in range(512)])  13.9 us
    all_gather x1, blocking collectives, shards(): lax.all_gather(pair, 'dev', axis=0, tiled=True, axis_index_groups=lines)  11.7 us
    all_to_all x1, starting transfers between devices, shards(): got1 = lax.all_to_all(send1, 'hst', 0, 0, tiled=True)  8.65 us
    unnamed x22, local copies, waits for them, and re-layouts  4.95 us
    pallas_call x1, Pallas kernels, shards(): pl.pallas_call(back_kernel, out_shape=shape((64, 128), BF16), grid_spec=p...  4.6 us
    pallas_call x1, Pallas kernels, shards(): pl.pallas_call(term_kernel, out_shape=[shape((4, 2, 16, 24, 128), F32)] *...  4.26 us
  transfers between devices with their start and end apart: 9, of which 4 were waited for; matrix products, arithmetic and copies ran while one was open for 4% of the time, Pallas kernels for 5%

profile of v2, /device:TPU:1, one launch (start us, length us, event | category | flops | bytes accessed | tf_op | source)
XLA Modules:
  0.0 103.0 jit_solution(388782880912817067)
XLA Ops:
  0.7 1.9 %copy-done = bf16[128,12288]{1,0:T(8,128)(2,1)S(1)} copy-done((bf16[128,12288]{1,0:T(8,128)(2,1)S(1)}, bf16[128,12288]{1,0:T(8,128)(2,1)}, u32[]{:S(2)}) %copy-start) | copy-done | bytes 3145752
  3.3 4.3 %shard_map.86 = (f32[4,2,16,24,128]{4,3,2,1,0:T(8,128)S(1)}, f32[4,2,16,24,128]{4,3,2,1,0:T(8,128)S(1)}) custom-call(s32[1]{0:T(128)} %bitcast.core_ref, bf16[64,128]{1,0:T(8,128)(2,1)S(1)} %bitcast.24, bf16[128,12288]{1,0:T(8,128)(2,1)S(1)} %copy-done, bf16[128,12288]{1,0:T(8,128)(2,1)S(1)} %copy-done, bf16[128,12288]{1,0:T(8,128)(2,1)S(1)} %copy-done, ...), custom_call_target="tpu_custom_call" | custom-call | tf_op jit(solution)/shard_map/pallas_call | solution.py:203
  7.5 8.8 %collective-permute-start = (f32[4,2,16,24,128]{4,3,2,1,0:T(8,128)S(1)}, f32[4,2,16,24,128]{4,3,2,1,0:T(8,128)}, u32[]{:S(2)}, u32[]{:S(2)}) collective-permute-start(f32[4,2,16,24,128]{4,3,2,1,0:T(8,128)S(1)} %get-tuple-element.12), channel_id=1, source_target_pairs={{0,8},{1,9},{2,10},{3,11},{4,12},{5,13},{6,14},{7,15},{8,0},{9,1},... | collective-permute-start | bytes 4718600 | tf_op jit(solution)/shard_map/ppermute | solution.py:193
  17.0 0.9 shard_map.85
  17.8 8.7 %all-to-all-start = ((bf16[64,24,128]{2,1,0:T(8,128)(2,1)}), bf16[64,24,128]{2,1,0:T(8,128)(2,1)S(1)}, u32[]{:S(2)}, u32[]{:S(2)}) async-start(bf16[64,24,128]{2,1,0:T(8,128)(2,1)} %shard_map.85), calls=%async_computation | async-start | bytes 786432 | tf_op jit(solution)/shard_map/all_to_all | solution.py:199
  26.5 1.4 %fusion.3 = (f16[2,16,24,128]{3,2,1,0:T(8,128)(2,1)S(1)}, f16[2,16,24,128]{3,2,1,0:T(8,128)(2,1)S(1)}, f16[2,16,24,128]{3,2,1,0:T(8,128)(2,1)S(1)}) fusion(f32[4,2,16,24,128]{4,3,2,1,0:T(8,128)} %collective-permute-done, s32[]{:T(128)S(6)} %select_n.46, f32[4,2,16,24,128]{4,3,2,1,0:T(8,128)S(1)} %get-tuple-element.11, s32[]{:T(128)S(6)} %select_n.47, ...), kind=kLoop, calls=%fused_computation.7 | loop fusion | flops 589824 | bytes 2949132 | tf_op jit(solution)/shard_map/convert_element_type | solution.py:220
  27.9 3.1 %collective-permute-start.1 = (f16[2,16,24,128]{3,2,1,0:T(8,128)(2,1)S(1)}, f16[2,16,24,128]{3,2,1,0:T(8,128)(2,1)S(1)}, u32[]{:S(2)}, u32[]{:S(2)}) collective-permute-start(f16[2,16,24,128]{3,2,1,0:T(8,128)(2,1)S(1)} %get-tuple-element.21), channel_id=1, source_target_pairs={{0,1},{1,0},{2,3},{3,2},{4,5},{5,4},{6,7},{7,6},{8,9},{9,8},{10,11... | collective-permute-start | bytes 589832 | tf_op jit(solution)/shard_map/ppermute | solution.py:193
  31.0 3.7 %collective-permute-start.3 = (f16[2,16,24,128]{3,2,1,0:T(8,128)(2,1)S(1)}, f16[2,16,24,128]{3,2,1,0:T(8,128)(2,1)S(1)}, u32[]{:S(2)}, u32[]{:S(2)}) collective-permute-start(f16[2,16,24,128]{3,2,1,0:T(8,128)(2,1)S(1)} %get-tuple-element.19), channel_id=1, source_target_pairs={{0,3},{1,2},{2,1},{3,0},{4,7},{5,6},{6,5},{7,4},{8,11},{9,10},{10,... | collective-permute-start | bytes 589832 | tf_op jit(solution)/shard_map/ppermute | solution.py:193
  34.8 2.6 %collective-permute-start.4 = (f16[2,16,24,128]{3,2,1,0:T(8,128)(2,1)S(1)}, f16[2,16,24,128]{3,2,1,0:T(8,128)(2,1)S(1)}, u32[]{:S(2)}, u32[]{:S(2)}) collective-permute-start(f16[2,16,24,128]{3,2,1,0:T(8,128)(2,1)S(1)} %get-tuple-element.20), channel_id=1, source_target_pairs={{0,2},{1,3},{2,0},{3,1},{4,6},{5,7},{6,4},{7,5},{8,10},{9,11},{10,... | collective-permute-start | bytes 589832 | tf_op jit(solution)/shard_map/ppermute | solution.py:193
  37.4 2.5 %collective-permute-done.3 = f16[2,16,24,128]{3,2,1,0:T(8,128)(2,1)S(1)} collective-permute-done((f16[2,16,24,128]{3,2,1,0:T(8,128)(2,1)S(1)}, f16[2,16,24,128]{3,2,1,0:T(8,128)(2,1)S(1)}, u32[]{:S(2)}, u32[]{:S(2)}) %collective-permute-start.3) | collective-permute-done | bytes 196640 | tf_op jit(solution)/shard_map/ppermute | solution.py:193
  39.8 3.8 %collective-permute-done.4 = f16[2,16,24,128]{3,2,1,0:T(8,128)(2,1)S(1)} collective-permute-done((f16[2,16,24,128]{3,2,1,0:T(8,128)(2,1)S(1)}, f16[2,16,24,128]{3,2,1,0:T(8,128)(2,1)S(1)}, u32[]{:S(2)}, u32[]{:S(2)}) %collective-permute-start.4) | collective-permute-done | bytes 196640 | tf_op jit(solution)/shard_map/ppermute | solution.py:193
  43.6 1.1 %fusion.1 = f32[2,16,24,128]{3,2,1,0:T(8,128)S(1)} fusion(f16[2,16,24,128]{3,2,1,0:T(8,128)(2,1)S(1)} %collective-permute-done.4, f16[2,16,24,128]{3,2,1,0:T(8,128)(2,1)S(1)} %collective-permute-done.3, f16[2,16,24,128]{3,2,1,0:T(8,128)(2,1)S(1)} %collective-permute-done.1, f32[4,2,16,24,128]{4,3,2,1,0:T(8,128)} %collective-permute-done, s32[]{:T(128)S(6)} %select_n.45, ...), kind=kLoop, calls=%fused_computation.2 | loop fusion | flops 688128 | bytes 1769476 | tf_op jit(solution)/shard_map/add | solution.py:225
  45.4 4.7 %collective-permute-start.5 = (f16[16,24,128]{2,1,0:T(8,128)(2,1)S(1)}, f16[16,24,128]{2,1,0:T(8,128)(2,1)S(1)}, u32[]{:S(2)}, u32[]{:S(2)}) collective-permute-start(f16[16,24,128]{2,1,0:T(8,128)(2,1)S(1)} %get-tuple-element.22), channel_id=1, source_target_pairs={{0,4},{1,5},{2,6},{3,7},{4,0},{5,1},{6,2},{7,3},{8,12},{9,13},{10,... | collective-permute-start | bytes 294920 | tf_op jit(solution)/shard_map/ppermute | solution.py:193
  50.4 4.4 %collective-permute-start.2 = (bf16[16,24,128]{2,1,0:T(8,128)(2,1)S(1)}, bf16[16,24,128]{2,1,0:T(8,128)(2,1)S(1)}, u32[]{:S(2)}, u32[]{:S(2)}) collective-permute-start(bf16[16,24,128]{2,1,0:T(8,128)(2,1)S(1)} %shard_map.87), channel_id=1, source_target_pairs={{0,4},{1,5},{2,6},{3,7},{4,0},{5,1},{6,2},{7,3},{8,12},{9,13},{10,... | collective-permute-start | bytes 294920 | tf_op jit(solution)/shard_map/ppermute | solution.py:193
  54.9 5.8 %collective-permute-done.2 = bf16[16,24,128]{2,1,0:T(8,128)(2,1)S(1)} collective-permute-done((bf16[16,24,128]{2,1,0:T(8,128)(2,1)S(1)}, bf16[16,24,128]{2,1,0:T(8,128)(2,1)S(1)}, u32[]{:S(2)}, u32[]{:S(2)}) %collective-permute-start.2) | collective-permute-done | bytes 98336 | tf_op jit(solution)/shard_map/ppermute | solution.py:193
  61.3 0.9 copy-done.3
  63.0 0.8 copy-done.2
  63.8 13.9 %all-to-all-start.1 = ((bf16[64,32,128]{2,1,0:T(8,128)(2,1)}), bf16[64,32,128]{2,1,0:T(8,128)(2,1)}, u32[]{:S(2)}, u32[]{:S(2)}) async-start(bf16[64,32,128]{2,1,0:T(8,128)(2,1)} %copy-done.2), calls=%async_computation.1 | async-start | bytes 1048576 | tf_op jit(solution)/shard_map/all_to_all | solution.py:238
  77.7 1.0 pad_maximum_fusion
  78.7 11.7 %all_gather.3 = bf16[3072,128]{1,0:T(8,128)(2,1)S(1)} all-gather(bf16[768,128]{1,0:T(8,128)(2,1)S(1)} %bitcast.26), channel_id=1, replica_groups={{0,1,2,3},{4,5,6,7},{8,9,10,11},{12,13,14,15},{16,17,18,19},{20,21,22,2..., dimensions={0}, use_global_device_ids=true | all-gather | bytes 983040 | tf_op jit(solution)/shard_map/all_gather | solution.py:248
  90.4 4.1 %collective-permute-start.6 = (bf16[4,2,16,24,128]{4,3,2,1,0:T(8,128)(2,1)S(1)}, bf16[4,2,16,24,128]{4,3,2,1,0:T(8,128)(2,1)S(1)}, u32[]{:S(2)}, u32[]{:S(2)}) collective-permute-start(bf16[4,2,16,24,128]{4,3,2,1,0:T(8,128)(2,1)S(1)} %bitcast.22), channel_id=1, source_target_pairs={{0,8},{1,9},{2,10},{3,11},{4,12},{5,13},{6,14},{7,15},{8,0},{9,1},... | collective-permute-start | bytes 2359304 | tf_op jit(solution)/shard_map/ppermute | solution.py:193
  94.5 1.8 %collective-permute-done.6.other_ref = bf16[4,2,16,24,128]{4,3,2,1,0:T(8,128)(2,1)S(1)} collective-permute-done((bf16[4,2,16,24,128]{4,3,2,1,0:T(8,128)(2,1)S(1)}, bf16[4,2,16,24,128]{4,3,2,1,0:T(8,128)(2,1)S(1)}, u32[]{:S(2)}, u32[]{:S(2)}) %collective-permute-start.6) | collective-permute-done | bytes 786464 | tf_op jit(solution)/shard_map/ppermute | solution.py:193
  96.4 4.6 %shard_map.90 = bf16[64,128]{1,0:T(8,128)(2,1)} custom-call(s32[2]{0:T(128)S(1)} %pad_add_fusion.place_ref, bf16[4,2,16,24,128]{4,3,2,1,0:T(8,128)(2,1)S(1)} %bitcast.23, bf16[4,2,16,24,128]{4,3,2,1,0:T(8,128)(2,1)S(1)} %collective-permute-done.6.other_ref, bf16[64,128]{1,0:T(8,128)(2,1)S(1)} %bitcast.25, bf16[128,12288]{1,0:T(8,128)(2,1)S(1)} %copy-done.1, ...), custom_call_target="tpu_custom_call" | custom-call | tf_op jit(solution)/shard_map/pallas_call | solution.py:252
  101.0 2.0 %shard_map.89 = (f32[3,2,256,128]{3,2,1,0:T(8,128)}, f32[24,64]{1,0:T(8,128)}) custom-call(bf16[64,32,128]{2,1,0:T(8,128)(2,1)} %all-to-all-done.1.got_ref), custom_call_target="tpu_custom_call" | custom-call | tf_op jit(solution)/shard_map/pallas_call | solution.py:239
  (30 shorter events, 3.1 us)
Async XLA Ops:
  0.6 1.9 %copy-start = (bf16[128,12288]{1,0:T(8,128)(2,1)S(1)}, bf16[128,12288]{1,0:T(8,128)(2,1)}, u32[]{:S(2)}) copy-start(bf16[128,12288]{1,0:T(8,128)(2,1)} %g3.3) | copy-start | bytes 9437188
  2.5 0.7 copy-start.6
  3.3 13.7 %copy-start.4 = (f32[3,320,128]{2,1,0:T(8,128)S(1)}, f32[3,320,128]{2,1,0:T(8,128)}, u32[]{:S(2)}) copy-start(f32[3,320,128]{2,1,0:T(8,128)} %states_ref.1) | copy-start | bytes 1474564
  3.3 13.7 %copy-start.8 = (bf16[24,64]{1,0:T(8,128)(2,1)S(1)}, bf16[24,64]{1,0:T(8,128)(2,1)}, u32[]{:S(2)}) copy-start(bf16[24,64]{1,0:T(8,128)(2,1)} %rows_ref.1) | copy-start | bytes 9220
  7.5 19.0 %collective-permute-start = (f32[4,2,16,24,128]{4,3,2,1,0:T(8,128)S(1)}, f32[4,2,16,24,128]{4,3,2,1,0:T(8,128)}, u32[]{:S(2)}, u32[]{:S(2)}) collective-permute-start(f32[4,2,16,24,128]{4,3,2,1,0:T(8,128)S(1)} %get-tuple-element.12), channel_id=1, source_target_pairs={{0,8},{1,9},{2,10},{3,11},{4,12},{5,13},{6,14},{7,15},{8,0},{9,1},... | collective-permute-start | bytes 4718600 | tf_op jit(solution)/shard_map/ppermute | solution.py:193
  17.8 32.4 %all-to-all-start = ((bf16[64,24,128]{2,1,0:T(8,128)(2,1)}), bf16[64,24,128]{2,1,0:T(8,128)(2,1)S(1)}, u32[]{:S(2)}, u32[]{:S(2)}) async-start(bf16[64,24,128]{2,1,0:T(8,128)(2,1)} %shard_map.85), calls=%async_computation | async-start | bytes 786432 | tf_op jit(solution)/shard_map/all_to_all | solution.py:199
  27.9 26.9 %copy-start.10 = (s32[64,2]{0,1:T(2,128)S(1)}, s32[64,2]{0,1:T(2,128)}, u32[]{:S(2)}) copy-start(s32[64,2]{0,1:T(2,128)} %param.10) | copy-start | bytes 1540
  27.9 9.5 %collective-permute-start.1 = (f16[2,16,24,128]{3,2,1,0:T(8,128)(2,1)S(1)}, f16[2,16,24,128]{3,2,1,0:T(8,128)(2,1)S(1)}, u32[]{:S(2)}, u32[]{:S(2)}) collective-permute-start(f16[2,16,24,128]{3,2,1,0:T(8,128)(2,1)S(1)} %get-tuple-element.21), channel_id=1, source_target_pairs={{0,1},{1,0},{2,3},{3,2},{4,5},{5,4},{6,7},{7,6},{8,9},{9,8},{10,11... | collective-permute-start | bytes 589832 | tf_op jit(solution)/shard_map/ppermute | solution.py:193
  31.0 8.8 %collective-permute-start.3 = (f16[2,16,24,128]{3,2,1,0:T(8,128)(2,1)S(1)}, f16[2,16,24,128]{3,2,1,0:T(8,128)(2,1)S(1)}, u32[]{:S(2)}, u32[]{:S(2)}) collective-permute-start(f16[2,16,24,128]{3,2,1,0:T(8,128)(2,1)S(1)} %get-tuple-element.19), channel_id=1, source_target_pairs={{0,3},{1,2},{2,1},{3,0},{4,7},{5,6},{6,5},{7,4},{8,11},{9,10},{10,... | collective-permute-start | bytes 589832 | tf_op jit(solution)/shard_map/ppermute | solution.py:193
  34.8 8.9 %collective-permute-start.4 = (f16[2,16,24,128]{3,2,1,0:T(8,128)(2,1)S(1)}, f16[2,16,24,128]{3,2,1,0:T(8,128)(2,1)S(1)}, u32[]{:S(2)}, u32[]{:S(2)}) collective-permute-start(f16[2,16,24,128]{3,2,1,0:T(8,128)(2,1)S(1)} %get-tuple-element.20), channel_id=1, source_target_pairs={{0,2},{1,3},{2,0},{3,1},{4,6},{5,7},{6,4},{7,5},{8,10},{9,11},{10,... | collective-permute-start | bytes 589832 | tf_op jit(solution)/shard_map/ppermute | solution.py:193
  45.4 15.3 %collective-permute-start.5 = (f16[16,24,128]{2,1,0:T(8,128)(2,1)S(1)}, f16[16,24,128]{2,1,0:T(8,128)(2,1)S(1)}, u32[]{:S(2)}, u32[]{:S(2)}) collective-permute-start(f16[16,24,128]{2,1,0:T(8,128)(2,1)S(1)} %get-tuple-element.22), channel_id=1, source_target_pairs={{0,4},{1,5},{2,6},{3,7},{4,0},{5,1},{6,2},{7,3},{8,12},{9,13},{10,... | collective-permute-start | bytes 294920 | tf_op jit(solution)/shard_map/ppermute | solution.py:193
  50.4 10.4 %copy-start.5 = (bf16[16,24,128]{2,1,0:T(8,128)(2,1)}, bf16[16,24,128]{2,1,0:T(8,128)(2,1)S(1)}, u32[]{:S(2)}) copy-start(bf16[16,24,128]{2,1,0:T(8,128)(2,1)S(1)} %shard_map.87) | copy-start | bytes 294916
  50.4 10.3 %collective-permute-start.2 = (bf16[16,24,128]{2,1,0:T(8,128)(2,1)S(1)}, bf16[16,24,128]{2,1,0:T(8,128)(2,1)S(1)}, u32[]{:S(2)}, u32[]{:S(2)}) collective-permute-start(bf16[16,24,128]{2,1,0:T(8,128)(2,1)S(1)} %shard_map.87), channel_id=1, source_target_pairs={{0,4},{1,5},{2,6},{3,7},{4,0},{5,1},{6,2},{7,3},{8,12},{9,13},{10,... | collective-permute-start | bytes 294920 | tf_op jit(solution)/shard_map/ppermute | solution.py:193
  60.7 0.6 copy-start.9
  61.3 0.9 copy-start.3
  62.3 34.1 %copy-start.1 = (bf16[128,12288]{1,0:T(8,128)(2,1)S(1)}, bf16[128,12288]{1,0:T(8,128)(2,1)}, u32[]{:S(2)}) copy-start(bf16[128,12288]{1,0:T(8,128)(2,1)} %g3.3) | copy-start | bytes 9437188
  62.3 34.1 %copy-start.7 = (bf16[128,64]{0,1:T(8,128)(2,1)S(1)}, bf16[128,64]{0,1:T(8,128)(2,1)}, u32[]{:S(2)}) copy-start(bf16[128,64]{0,1:T(8,128)(2,1)} %param.7) | copy-start | bytes 49156
  63.0 0.8 copy-start.2
  63.8 37.2 %all-to-all-start.1 = ((bf16[64,32,128]{2,1,0:T(8,128)(2,1)}), bf16[64,32,128]{2,1,0:T(8,128)(2,1)}, u32[]{:S(2)}, u32[]{:S(2)}) async-start(bf16[64,32,128]{2,1,0:T(8,128)(2,1)} %copy-done.2), calls=%async_computation.1 | async-start | bytes 1048576 | tf_op jit(solution)/shard_map/all_to_all | solution.py:238
  90.4 6.0 %collective-permute-start.6 = (bf16[4,2,16,24,128]{4,3,2,1,0:T(8,128)(2,1)S(1)}, bf16[4,2,16,24,128]{4,3,2,1,0:T(8,128)(2,1)S(1)}, u32[]{:S(2)}, u32[]{:S(2)}) collective-permute-start(bf16[4,2,16,24,128]{4,3,2,1,0:T(8,128)(2,1)S(1)} %bitcast.22), channel_id=1, source_target_pairs={{0,8},{1,9},{2,10},{3,11},{4,12},{5,13},{6,14},{7,15},{8,0},{9,1},... | collective-permute-start | bytes 2359304 | tf_op jit(solution)/shard_map/ppermute | solution.py:193

commit v3 on v2

--- a/solution.py
+++ b/solution.py
@@ -219,7 +219,7 @@
 
     leaving = [pick(k).astype(jnp.float16) for k in (1, 3, 2)]
     parts = [flip(part, k) for part, k in zip(leaving, (1, 3, 2))]
-    got1, _ = lax.optimization_barrier((got1, parts[0]))
+    got1, _ = lax.optimization_barrier((got1, leaving))
     summed = pick(0)
     for part in parts:
         summed = summed + part.astype(F32)
@@ -230,6 +230,7 @@
     matches = partner_hosts[:, :, None] == sources[None, None, :]
     inverse = jnp.sum(jnp.where(matches, sources[:, None, None], 0), axis=0)
     held = call(weight_kernel, shape((16, 24, 128), BF16), [VMEM])(got1)
+    held, _ = lax.optimization_barrier((held, parts[0]))
     across = flip(held, 4)
     inverse, _ = lax.optimization_barrier((inverse, across))
     send2 = call(second_kernel, shape((64, 32, 128), BF16), [SMEM, VMEM, VMEM, VMEM])(

time: 104 us -> 101 us (0.971)
  local copies, waits for them, and re-layouts: 4.95 us -> 3.42 us
  waiting for transfers between devices: 13.9 us -> 12.8 us
    ppermute x7, waiting for transfers between devices: 13.9 us -> 7.57 us  [flip(): return lax.ppermute(array, axes, [(i, i ^ bits) for i in range(512)])]
    all_to_all x1, waiting for transfers between devices: 0.01 us -> 5.23 us  [shards(): got1 = lax.all_to_all(send1, 'hst', 0, 0, tiled=True)]
    unnamed x22 -> x18, local copies, waits for them, and re-layouts: 4.95 us -> 3.42 us
  transfers between devices with their start and end apart: 9 -> 9, of which waited for: 4 -> 4; matrix products, arithmetic and copies ran while one was open for 4% -> 2% of each run, Pallas kernels for 5% -> 6%
where the time goes in v3:
time: 101 us
  starting transfers between devices  55 us (54%)
  waiting for transfers between devices  12.8 us (13%)
  Pallas kernels  12.6 us (12%)
  blocking collectives  11.7 us (12%)
  other arithmetic  3.64 us (4%)
  local copies, waits for them, and re-layouts  3.42 us (3%)
  between operations  1.57 us (2%)
    ppermute x7, starting transfers between devices, flip(): return lax.ppermute(array, axes, [(i, i ^ bits) for i in range(512)])  31.5 us
    all_to_all x1, starting transfers between devices, shards(): got2 = lax.all_to_all(send2, 'hst', 0, 0, tiled=True)  14.9 us
    all_gather x1, blocking collectives, shards(): lax.all_gather(pair, 'dev', axis=0, tiled=True, axis_index_groups=lines)  11.7 us
    all_to_all x1, starting transfers between devices, shards(): got1 = lax.all_to_all(send1, 'hst', 0, 0, tiled=True)  8.65 us
    ppermute x7, waiting for transfers between devices, flip(): return lax.ppermute(array, axes, [(i, i ^ bits) for i in range(512)])  7.57 us
    all_to_all x1, waiting for transfers between devices, shards(): got1 = lax.all_to_all(send1, 'hst', 0, 0, tiled=True)  5.23 us
    pallas_call x1, Pallas kernels, shards(): pl.pallas_call(back_kernel, out_shape=shape((64, 128), BF16), grid_spec=p...  4.6 us
    pallas_call x1, Pallas kernels, shards(): pl.pallas_call(term_kernel, out_shape=[shape((4, 2, 16, 24, 128), F32)] *...  4.26 us
  transfers between devices with their start and end apart: 9, of which 4 were waited for; matrix products, arithmetic and copies ran while one was open for 2% of the time, Pallas kernels for 6%

profile of v3, /device:TPU:1, one launch (start us, length us, event | category | flops | bytes accessed | tf_op | source)
XLA Modules:
  0.0 100.8 jit_solution(13111639974653429556)
XLA Ops:
  0.7 1.9 %copy-done = bf16[128,12288]{1,0:T(8,128)(2,1)S(1)} copy-done((bf16[128,12288]{1,0:T(8,128)(2,1)S(1)}, bf16[128,12288]{1,0:T(8,128)(2,1)}, u32[]{:S(2)}) %copy-start) | copy-done | bytes 3145752
  3.3 4.3 %shard_map.86 = (f32[4,2,16,24,128]{4,3,2,1,0:T(8,128)S(1)}, f32[4,2,16,24,128]{4,3,2,1,0:T(8,128)S(1)}) custom-call(s32[1]{0:T(128)} %bitcast.core_ref, bf16[64,128]{1,0:T(8,128)(2,1)S(1)} %bitcast.24, bf16[128,12288]{1,0:T(8,128)(2,1)S(1)} %copy-done, bf16[128,12288]{1,0:T(8,128)(2,1)S(1)} %copy-done, bf16[128,12288]{1,0:T(8,128)(2,1)S(1)} %copy-done, ...), custom_call_target="tpu_custom_call" | custom-call | tf_op jit(solution)/shard_map/pallas_call | solution.py:203
  7.5 8.8 %collective-permute-start = (f32[4,2,16,24,128]{4,3,2,1,0:T(8,128)S(1)}, f32[4,2,16,24,128]{4,3,2,1,0:T(8,128)}, u32[]{:S(2)}, u32[]{:S(2)}) collective-permute-start(f32[4,2,16,24,128]{4,3,2,1,0:T(8,128)S(1)} %get-tuple-element.13), channel_id=1, source_target_pairs={{0,8},{1,9},{2,10},{3,11},{4,12},{5,13},{6,14},{7,15},{8,0},{9,1},... | collective-permute-start | bytes 4718600 | tf_op jit(solution)/shard_map/ppermute | solution.py:193
  17.0 0.9 shard_map.85
  17.8 8.7 %all-to-all-start = ((bf16[64,24,128]{2,1,0:T(8,128)(2,1)}), bf16[64,24,128]{2,1,0:T(8,128)(2,1)S(1)}, u32[]{:S(2)}, u32[]{:S(2)}) async-start(bf16[64,24,128]{2,1,0:T(8,128)(2,1)} %shard_map.85), calls=%async_computation | async-start | bytes 786432 | tf_op jit(solution)/shard_map/all_to_all | solution.py:199
  26.5 1.4 %fusion.4 = (f16[2,16,24,128]{3,2,1,0:T(8,128)(2,1)S(1)}, f16[2,16,24,128]{3,2,1,0:T(8,128)(2,1)S(1)}, f16[2,16,24,128]{3,2,1,0:T(8,128)(2,1)S(1)}) fusion(f32[4,2,16,24,128]{4,3,2,1,0:T(8,128)} %collective-permute-done, s32[]{:T(128)S(6)} %select_n.46, f32[4,2,16,24,128]{4,3,2,1,0:T(8,128)S(1)} %get-tuple-element.12, s32[]{:T(128)S(6)} %select_n.45, ...), kind=kLoop, calls=%fused_computation.8 | loop fusion | flops 589824 | bytes 2949132 | tf_op jit(solution)/shard_map/convert_element_type | solution.py:220
  27.9 3.1 %collective-permute-start.1 = (f16[2,16,24,128]{3,2,1,0:T(8,128)(2,1)S(1)}, f16[2,16,24,128]{3,2,1,0:T(8,128)(2,1)S(1)}, u32[]{:S(2)}, u32[]{:S(2)}) collective-permute-start(f16[2,16,24,128]{3,2,1,0:T(8,128)(2,1)S(1)} %get-tuple-element.23), channel_id=1, source_target_pairs={{0,1},{1,0},{2,3},{3,2},{4,5},{5,4},{6,7},{7,6},{8,9},{9,8},{10,11... | collective-permute-start | bytes 589832 | tf_op jit(solution)/shard_map/ppermute | solution.py:193
  31.0 3.7 %collective-permute-start.3 = (f16[2,16,24,128]{3,2,1,0:T(8,128)(2,1)S(1)}, f16[2,16,24,128]{3,2,1,0:T(8,128)(2,1)S(1)}, u32[]{:S(2)}, u32[]{:S(2)}) collective-permute-start(f16[2,16,24,128]{3,2,1,0:T(8,128)(2,1)S(1)} %get-tuple-element.22), channel_id=1, source_target_pairs={{0,3},{1,2},{2,1},{3,0},{4,7},{5,6},{6,5},{7,4},{8,11},{9,10},{10,... | collective-permute-start | bytes 589832 | tf_op jit(solution)/shard_map/ppermute | solution.py:193
  34.8 2.6 %collective-permute-start.4 = (f16[2,16,24,128]{3,2,1,0:T(8,128)(2,1)S(1)}, f16[2,16,24,128]{3,2,1,0:T(8,128)(2,1)S(1)}, u32[]{:S(2)}, u32[]{:S(2)}) collective-permute-start(f16[2,16,24,128]{3,2,1,0:T(8,128)(2,1)S(1)} %get-tuple-element.21), channel_id=1, source_target_pairs={{0,2},{1,3},{2,0},{3,1},{4,6},{5,7},{6,4},{7,5},{8,10},{9,11},{10,... | collective-permute-start | bytes 589832 | tf_op jit(solution)/shard_map/ppermute | solution.py:193
  37.4 5.2 %all-to-all-done.got_ref = bf16[64,24,128]{2,1,0:T(8,128)(2,1)S(1)} async-done(((bf16[64,24,128]{2,1,0:T(8,128)(2,1)}), bf16[64,24,128]{2,1,0:T(8,128)(2,1)S(1)}, u32[]{:S(2)}, u32[]{:S(2)}) %all-to-all-start) | async-done | bytes 393248 | tf_op jit(solution)/shard_map/all_to_all | solution.py:199
  42.8 0.9 collective-permute-done.4
  43.6 1.1 %fusion.1 = f32[2,16,24,128]{3,2,1,0:T(8,128)S(1)} fusion(f16[2,16,24,128]{3,2,1,0:T(8,128)(2,1)S(1)} %collective-permute-done.4, f16[2,16,24,128]{3,2,1,0:T(8,128)(2,1)S(1)} %collective-permute-done.3, f16[2,16,24,128]{3,2,1,0:T(8,128)(2,1)S(1)} %collective-permute-done.1, f32[4,2,16,24,128]{4,3,2,1,0:T(8,128)} %collective-permute-done, s32[]{:T(128)S(6)} %select_n.47, ...), kind=kLoop, calls=%fused_computation.2 | loop fusion | flops 688128 | bytes 1769476 | tf_op jit(solution)/shard_map/add | solution.py:225
  44.8 4.8 %collective-permute-start.5 = (f16[16,24,128]{2,1,0:T(8,128)(2,1)S(1)}, f16[16,24,128]{2,1,0:T(8,128)(2,1)S(1)}, u32[]{:S(2)}, u32[]{:S(2)}) collective-permute-start(f16[16,24,128]{2,1,0:T(8,128)(2,1)S(1)} %get-tuple-element.24), channel_id=1, source_target_pairs={{0,4},{1,5},{2,6},{3,7},{4,0},{5,1},{6,2},{7,3},{8,12},{9,13},{10,... | collective-permute-start | bytes 294920 | tf_op jit(solution)/shard_map/ppermute | solution.py:193
  49.5 4.4 %collective-permute-start.2 = (bf16[16,24,128]{2,1,0:T(8,128)(2,1)S(1)}, bf16[16,24,128]{2,1,0:T(8,128)(2,1)}, u32[]{:S(2)}, u32[]{:S(2)}) collective-permute-start(bf16[16,24,128]{2,1,0:T(8,128)(2,1)S(1)} %shard_map.87), channel_id=1, source_target_pairs={{0,4},{1,5},{2,6},{3,7},{4,0},{5,1},{6,2},{7,3},{8,12},{9,13},{10,... | collective-permute-start | bytes 294920 | tf_op jit(solution)/shard_map/ppermute | solution.py:193
  54.1 4.9 %collective-permute-done.2 = bf16[16,24,128]{2,1,0:T(8,128)(2,1)} collective-permute-done((bf16[16,24,128]{2,1,0:T(8,128)(2,1)S(1)}, bf16[16,24,128]{2,1,0:T(8,128)(2,1)}, u32[]{:S(2)}, u32[]{:S(2)}) %collective-permute-start.2) | collective-permute-done | bytes 98336 | tf_op jit(solution)/shard_map/ppermute | solution.py:193
  59.1 0.7 shard_map.88
  59.8 0.8 copy-done.2
  60.6 14.9 %all-to-all-start.1 = ((bf16[64,32,128]{2,1,0:T(8,128)(2,1)}), bf16[64,32,128]{2,1,0:T(8,128)(2,1)}, u32[]{:S(2)}, u32[]{:S(2)}) async-start(bf16[64,32,128]{2,1,0:T(8,128)(2,1)} %copy-done.2), calls=%async_computation.1 | async-start | bytes 1048576 | tf_op jit(solution)/shard_map/all_to_all | solution.py:239
  75.5 1.0 pad_maximum_fusion
  76.4 11.7 %all_gather.3 = bf16[3072,128]{1,0:T(8,128)(2,1)S(1)} all-gather(bf16[768,128]{1,0:T(8,128)(2,1)S(1)} %bitcast.26), channel_id=1, replica_groups={{0,1,2,3},{4,5,6,7},{8,9,10,11},{12,13,14,15},{16,17,18,19},{20,21,22,2..., dimensions={0}, use_global_device_ids=true | all-gather | bytes 983040 | tf_op jit(solution)/shard_map/all_gather | solution.py:249
  88.1 4.1 %collective-permute-start.6 = (bf16[4,2,16,24,128]{4,3,2,1,0:T(8,128)(2,1)S(1)}, bf16[4,2,16,24,128]{4,3,2,1,0:T(8,128)(2,1)S(1)}, u32[]{:S(2)}, u32[]{:S(2)}) collective-permute-start(bf16[4,2,16,24,128]{4,3,2,1,0:T(8,128)(2,1)S(1)} %bitcast.22), channel_id=1, source_target_pairs={{0,8},{1,9},{2,10},{3,11},{4,12},{5,13},{6,14},{7,15},{8,0},{9,1},... | collective-permute-start | bytes 2359304 | tf_op jit(solution)/shard_map/ppermute | solution.py:193
  92.3 1.8 %collective-permute-done.6.other_ref = bf16[4,2,16,24,128]{4,3,2,1,0:T(8,128)(2,1)S(1)} collective-permute-done((bf16[4,2,16,24,128]{4,3,2,1,0:T(8,128)(2,1)S(1)}, bf16[4,2,16,24,128]{4,3,2,1,0:T(8,128)(2,1)S(1)}, u32[]{:S(2)}, u32[]{:S(2)}) %collective-permute-start.6) | collective-permute-done | bytes 786464 | tf_op jit(solution)/shard_map/ppermute | solution.py:193
  94.1 4.6 %shard_map.90 = bf16[64,128]{1,0:T(8,128)(2,1)} custom-call(s32[2]{0:T(128)S(1)} %pad_add_fusion.place_ref, bf16[4,2,16,24,128]{4,3,2,1,0:T(8,128)(2,1)S(1)} %bitcast.23, bf16[4,2,16,24,128]{4,3,2,1,0:T(8,128)(2,1)S(1)} %collective-permute-done.6.other_ref, bf16[64,128]{1,0:T(8,128)(2,1)S(1)} %bitcast.25, bf16[128,12288]{1,0:T(8,128)(2,1)S(1)} %copy-done.1, ...), custom_call_target="tpu_custom_call" | custom-call | tf_op jit(solution)/shard_map/pallas_call | solution.py:253
  98.7 2.0 %shard_map.89 = (f32[3,2,256,128]{3,2,1,0:T(8,128)}, f32[24,64]{1,0:T(8,128)}) custom-call(bf16[64,32,128]{2,1,0:T(8,128)(2,1)} %all-to-all-done.1.got_ref), custom_call_target="tpu_custom_call" | custom-call | tf_op jit(solution)/shard_map/pallas_call | solution.py:240
  (26 shorter events, 1.2 us)
Async XLA Ops:
  0.6 1.9 %copy-start = (bf16[128,12288]{1,0:T(8,128)(2,1)S(1)}, bf16[128,12288]{1,0:T(8,128)(2,1)}, u32[]{:S(2)}) copy-start(bf16[128,12288]{1,0:T(8,128)(2,1)} %g3.3) | copy-start | bytes 9437188
  2.5 0.7 copy-start.5
  3.3 13.7 %copy-start.3 = (f32[3,320,128]{2,1,0:T(8,128)S(1)}, f32[3,320,128]{2,1,0:T(8,128)}, u32[]{:S(2)}) copy-start(f32[3,320,128]{2,1,0:T(8,128)} %states_ref.1) | copy-start | bytes 1474564
  3.3 13.7 %copy-start.7 = (bf16[24,64]{1,0:T(8,128)(2,1)S(1)}, bf16[24,64]{1,0:T(8,128)(2,1)}, u32[]{:S(2)}) copy-start(bf16[24,64]{1,0:T(8,128)(2,1)} %rows_ref.1) | copy-start | bytes 9220
  7.5 19.0 %collective-permute-start = (f32[4,2,16,24,128]{4,3,2,1,0:T(8,128)S(1)}, f32[4,2,16,24,128]{4,3,2,1,0:T(8,128)}, u32[]{:S(2)}, u32[]{:S(2)}) collective-permute-start(f32[4,2,16,24,128]{4,3,2,1,0:T(8,128)S(1)} %get-tuple-element.13), channel_id=1, source_target_pairs={{0,8},{1,9},{2,10},{3,11},{4,12},{5,13},{6,14},{7,15},{8,0},{9,1},... | collective-permute-start | bytes 4718600 | tf_op jit(solution)/shard_map/ppermute | solution.py:193
  17.8 24.8 %all-to-all-start = ((bf16[64,24,128]{2,1,0:T(8,128)(2,1)}), bf16[64,24,128]{2,1,0:T(8,128)(2,1)S(1)}, u32[]{:S(2)}, u32[]{:S(2)}) async-start(bf16[64,24,128]{2,1,0:T(8,128)(2,1)} %shard_map.85), calls=%async_computation | async-start | bytes 786432 | tf_op jit(solution)/shard_map/all_to_all | solution.py:199
  27.9 26.1 %copy-start.8 = (s32[64,2]{0,1:T(2,128)S(1)}, s32[64,2]{0,1:T(2,128)}, u32[]{:S(2)}) copy-start(s32[64,2]{0,1:T(2,128)} %param.10) | copy-start | bytes 1540
  27.9 14.9 %collective-permute-start.1 = (f16[2,16,24,128]{3,2,1,0:T(8,128)(2,1)S(1)}, f16[2,16,24,128]{3,2,1,0:T(8,128)(2,1)S(1)}, u32[]{:S(2)}, u32[]{:S(2)}) collective-permute-start(f16[2,16,24,128]{3,2,1,0:T(8,128)(2,1)S(1)} %get-tuple-element.23), channel_id=1, source_target_pairs={{0,1},{1,0},{2,3},{3,2},{4,5},{5,4},{6,7},{7,6},{8,9},{9,8},{10,11... | collective-permute-start | bytes 589832 | tf_op jit(solution)/shard_map/ppermute | solution.py:193
  31.0 11.7 %collective-permute-start.3 = (f16[2,16,24,128]{3,2,1,0:T(8,128)(2,1)S(1)}, f16[2,16,24,128]{3,2,1,0:T(8,128)(2,1)S(1)}, u32[]{:S(2)}, u32[]{:S(2)}) collective-permute-start(f16[2,16,24,128]{3,2,1,0:T(8,128)(2,1)S(1)} %get-tuple-element.22), channel_id=1, source_target_pairs={{0,3},{1,2},{2,1},{3,0},{4,7},{5,6},{6,5},{7,4},{8,11},{9,10},{10,... | collective-permute-start | bytes 589832 | tf_op jit(solution)/shard_map/ppermute | solution.py:193
  34.8 8.9 %collective-permute-start.4 = (f16[2,16,24,128]{3,2,1,0:T(8,128)(2,1)S(1)}, f16[2,16,24,128]{3,2,1,0:T(8,128)(2,1)S(1)}, u32[]{:S(2)}, u32[]{:S(2)}) collective-permute-start(f16[2,16,24,128]{3,2,1,0:T(8,128)(2,1)S(1)} %get-tuple-element.21), channel_id=1, source_target_pairs={{0,2},{1,3},{2,0},{3,1},{4,6},{5,7},{6,4},{7,5},{8,10},{9,11},{10,... | collective-permute-start | bytes 589832 | tf_op jit(solution)/shard_map/ppermute | solution.py:193
  42.8 16.3 %copy-start.4 = (bf16[16,24,128]{2,1,0:T(8,128)(2,1)}, bf16[16,24,128]{2,1,0:T(8,128)(2,1)S(1)}, u32[]{:S(2)}) copy-start(bf16[16,24,128]{2,1,0:T(8,128)(2,1)S(1)} %shard_map.87) | copy-start | bytes 294916
  44.8 14.2 %collective-permute-start.5 = (f16[16,24,128]{2,1,0:T(8,128)(2,1)S(1)}, f16[16,24,128]{2,1,0:T(8,128)(2,1)S(1)}, u32[]{:S(2)}, u32[]{:S(2)}) collective-permute-start(f16[16,24,128]{2,1,0:T(8,128)(2,1)S(1)} %get-tuple-element.24), channel_id=1, source_target_pairs={{0,4},{1,5},{2,6},{3,7},{4,0},{5,1},{6,2},{7,3},{8,12},{9,13},{10,... | collective-permute-start | bytes 294920 | tf_op jit(solution)/shard_map/ppermute | solution.py:193
  49.5 9.5 %collective-permute-start.2 = (bf16[16,24,128]{2,1,0:T(8,128)(2,1)S(1)}, bf16[16,24,128]{2,1,0:T(8,128)(2,1)}, u32[]{:S(2)}, u32[]{:S(2)}) collective-permute-start(bf16[16,24,128]{2,1,0:T(8,128)(2,1)S(1)} %shard_map.87), channel_id=1, source_target_pairs={{0,4},{1,5},{2,6},{3,7},{4,0},{5,1},{6,2},{7,3},{8,12},{9,13},{10,... | collective-permute-start | bytes 294920 | tf_op jit(solution)/shard_map/ppermute | solution.py:193
  59.0 35.1 %copy-start.1 = (bf16[128,12288]{1,0:T(8,128)(2,1)S(1)}, bf16[128,12288]{1,0:T(8,128)(2,1)}, u32[]{:S(2)}) copy-start(bf16[128,12288]{1,0:T(8,128)(2,1)} %g3.3) | copy-start | bytes 9437188
  59.0 35.1 %copy-start.6 = (bf16[128,64]{0,1:T(8,128)(2,1)S(1)}, bf16[128,64]{0,1:T(8,128)(2,1)}, u32[]{:S(2)}) copy-start(bf16[128,64]{0,1:T(8,128)(2,1)} %param.7) | copy-start | bytes 49156
  59.8 0.8 copy-start.2
  60.6 38.2 %all-to-all-start.1 = ((bf16[64,32,128]{2,1,0:T(8,128)(2,1)}), bf16[64,32,128]{2,1,0:T(8,128)(2,1)}, u32[]{:S(2)}, u32[]{:S(2)}) async-start(bf16[64,32,128]{2,1,0:T(8,128)(2,1)} %copy-done.2), calls=%async_computation.1 | async-start | bytes 1048576 | tf_op jit(solution)/shard_map/all_to_all | solution.py:239
  88.1 6.0 %collective-permute-start.6 = (bf16[4,2,16,24,128]{4,3,2,1,0:T(8,128)(2,1)S(1)}, bf16[4,2,16,24,128]{4,3,2,1,0:T(8,128)(2,1)S(1)}, u32[]{:S(2)}, u32[]{:S(2)}) collective-permute-start(bf16[4,2,16,24,128]{4,3,2,1,0:T(8,128)(2,1)S(1)} %bitcast.22), channel_id=1, source_target_pairs={{0,8},{1,9},{2,10},{3,11},{4,12},{5,13},{6,14},{7,15},{8,0},{9,1},... | collective-permute-start | bytes 2359304 | tf_op jit(solution)/shard_map/ppermute | solution.py:193
